TPU v7x, 128 devices: a whole 4x4x4 slice. The times are simulated.
128 devices in a mesh: station: 8 (over x, core), tm: 16 (over z, y).
Axes of the slice: x: 4, y: 4, z: 4, core: 2. Of those that a mesh axis runs over, the one named last changes fastest.
Arguments:
- voltages: bfloat16 [512, 512, 2, 1024], P('station', 'tm'), may hold values from -6 to 6
- taps: float32 [16, 1024], replicated, may hold values from -1.5 to 1.5
Outputs:
- visibilities: float32 [1024, 2, 512, 512], P(('station', 'tm'))
All inputs are finite; a program needn't handle non-finite values.
Results may differ from a plain program's by a relative error of at most 0.0047.
Values may be sent and summed in bfloat16 or wider, within the bound.
No kernel may reach another device: no remote copies, remote signals or barrier semaphores. Data moves between devices by JAX's collectives and lax.ppermute only.
A program may use at most 192 MiB of HBM per device.

v0:
```python
import math

import jax
import jax.numpy as jnp
from jax import lax
from jax.sharding import PartitionSpec as P


def passed_along(value, axis, steps):
    count = lax.axis_size(axis)
    leading, last = (max(0, -steps), min(count, count - steps))
    return lax.ppermute(value, axis, [(source, source + steps) for source in range(leading, last)])


def dft_parts(nfft):
    index = jnp.arange(nfft, dtype=jnp.int32)
    product = index[:, None] * index[None, :] % nfft
    angle = 2.0 * math.pi / nfft * product.astype(jnp.float32)
    return (jnp.cos(angle) / math.sqrt(nfft), jnp.sin(angle) / math.sqrt(nfft))


def assemble(cos_t, sin_t):
    upper = jnp.concatenate([cos_t, -sin_t], axis=1)
    lower = jnp.concatenate([sin_t, cos_t], axis=1)
    return jnp.concatenate([upper, lower], axis=0).astype(jnp.bfloat16)


def correlate_block(left, right_left, right_twist):
    right = jnp.stack([right_left, right_twist], axis=1)
    return jnp.einsum("cit,crjt->crij", left, right, preferred_element_type=jnp.float32)


def per_device(voltages, taps):
    inputs_here = voltages.shape[0]
    frames = voltages.shape[1]
    nfft = voltages.shape[3]
    tap_count = taps.shape[0]
    n_station = lax.axis_size("station")
    n_tm = lax.axis_size("tm")
    tail = passed_along(voltages[:, frames - (tap_count - 1) :], "tm", 1)
    extended = jnp.concatenate([tail, voltages], axis=1)
    total = jnp.zeros(voltages.shape, jnp.float32)
    for k in range(tap_count):
        start = tap_count - 1 - k
        total = total + taps[k][None, None, None, :] * extended[:, start : start + frames].astype(
            jnp.float32
        )
    filtered = total.astype(jnp.bfloat16).reshape(-1, 2 * nfft)
    cos_t, sin_t = dft_parts(nfft)
    table = assemble(cos_t, sin_t)
    spectra = jnp.dot(filtered, table, preferred_element_type=jnp.float32).astype(jnp.bfloat16)
    spectra = spectra.reshape(inputs_here, frames, 2, nfft)
    channels = nfft // (n_station * n_tm)
    turned = lax.all_to_all(
        lax.all_to_all(spectra, "station", split_axis=3, concat_axis=0, tiled=True),
        "tm",
        split_axis=3,
        concat_axis=1,
        tiled=True,
    )
    all_inputs = turned.shape[0]
    all_frames = turned.shape[1]
    ordered = jnp.transpose(turned, (3, 0, 2, 1))
    left = ordered.reshape(channels, all_inputs, 2 * all_frames)
    twisted = jnp.concatenate([-ordered[:, :, 1, :], ordered[:, :, 0, :]], axis=-1)
    summed = correlate_block(left, left, twisted)
    return summed * (1.0 / all_frames)


def solution(mesh):
    return jax.shard_map(
        per_device,
        mesh=mesh,
        in_specs=(P("station", "tm", None, None), P()),
        out_specs=P(("station", "tm"), None, None, None),
        check_vma=False,
    )
```

profile of v0, /device:TPU:7, one launch (start us, length us, event | category | flops | bytes accessed | tf_op | source)
XLA Modules:
  0.0 725.5 jit_solution(3675107932185699572)
XLA Ops:
  13.7 16.5 %fusion.25 = bf16[1024,1024]{1,0:T(8,128)(2,1)} fusion(), kind=kLoop, calls=%fused_computation.32 | loop fusion | flops 16777216 | bytes 2097152 | tf_op jit(solution)/shard_map/convert.2
  30.3 18.0 %negate_convert_fusion = (bf16[1024,1024]{1,0:T(8,128)(2,1)}, bf16[1024,1024]{1,0:T(8,128)(2,1)}) fusion(), kind=kLoop, calls=%fused_computation.26 | loop fusion | flops 19922944 | bytes 4194304 | tf_op jit(solution)/shard_map/convert.5
  48.3 45.8 %collective-permute-done = bf16[64,15,2,1024]{3,2,1,0:T(2,128)(2,1)} collective-permute-done((bf16[64,15,2,1024]{3,2,1,0:T(2,128)(2,1)}, bf16[64,15,2,1024]{3,2,1,0:T(2,128)(2,1)}, u32[]{:S(2)}, u32[]{:S(2)}) %collective-permute-start) | collective-permute-done | bytes 3932192 | tf_op jit(solution)/shard_map/ppermute | solution.py:12
  100.7 7.0 constant_dynamic-update-slice_fusion
  107.7 129.2 %add_convert_fusion = bf16[64,32,2,1024]{3,2,1,0:T(2,128)(2,1)} fusion(bf16[64,32,2,1024]{3,2,1,0:T(2,128)(2,1)S(1)} %bitcast.53, bf16[64,47,2,1024]{3,2,1,0:T(2,128)(2,1)} %constant_dynamic-update-slice_fusion, f32[1024]{0:T(1024)S(1)} %bitcast.74, f32[1024]{0:T(1024)S(1)} %bitcast.75, f32[1024]{0:T(1024)S(1)} %bitcast.61, f32[1024]{0:T(1024)S(1)} %bitcast.62, ...), kind=kLoop, calls=%fused_computation.5 | loop fusion | flops 201326592 | bytes 142671872 | tf_op jit(solution)/shard_map/convert_element_type | solution.py:48
  236.9 10.5 %copy.49 = bf16[256,8,2,1024]{3,1,2,0:T(8,128)(2,1)} copy(bf16[256,8,2,1024]{3,2,1,0:T(2,128)(2,1)} %bitcast.54) | data formatting | bytes 16777216
  247.4 26.2 %fusion.15 = bf16[2048,2048]{1,0:T(8,128)(2,1)} fusion(bf16[2048,2048]{1,0:T(8,128)(2,1)} %bitcast.59, bf16[1024,1024]{1,0:T(8,128)(2,1)} %get-tuple-element.24, bf16[1024,1024]{1,0:T(8,128)(2,1)S(1)} %copy-done, bf16[1024,1024]{1,0:T(8,128)(2,1)} %get-tuple-element.23), kind=kOutput, calls=%fused_computation.16 | convolution fusion | flops 17217617920 | bytes 23068672 | tf_op jit(solution)/shard_map/dot_general | solution.py:51
  273.6 14.5 %reshape.27 = bf16[64,32,2,1024]{3,2,1,0:T(2,128)(2,1)} reshape(bf16[2048,2048]{1,0:T(8,128)(2,1)} %fusion.15) | data formatting | bytes 16777216 | tf_op jit(solution)/shard_map/reshape | solution.py:52
  288.1 28.3 %copy.32 = bf16[64,32,2,1024]{0,1,2,3:T(8,128)(2,1)} copy(bf16[64,32,2,1024]{3,2,1,0:T(2,128)(2,1)} %reshape.27) | data formatting | bytes 16777216 | tf_op jit(solution)/shard_map/reshape | solution.py:52
  316.4 16.9 %reshape.31 = bf16[8,2,262144]{2,1,0:T(2,128)(2,1)} reshape(bf16[1024,2,32,64]{3,2,1,0:T(8,128)(2,1)} %bitcast.50) | data formatting | bytes 16777216
  333.3 100.6 %all_to_all.36 = bf16[8,2,262144]{2,1,0:T(2,128)(2,1)} all-to-all(bf16[8,2,262144]{2,1,0:T(2,128)(2,1)} %reshape.31), channel_id=1, replica_groups=mesh['station'=8,'tm'=16] {'station'}, dimensions={0} | all-to-all | bytes 16777216 | tf_op jit(solution)/shard_map/all_to_all | solution.py:55
  433.9 16.5 %reshape.32 = bf16[1024,2,32,64]{3,2,1,0:T(8,128)(2,1)} reshape(bf16[8,2,262144]{2,1,0:T(2,128)(2,1)} %all_to_all.36) | data formatting | bytes 16777216
  450.4 27.7 %copy.34 = bf16[8,64,32,2,128]{4,2,3,1,0:T(8,128)(2,1)} copy(bf16[8,64,32,2,128]{1,2,3,4,0:T(8,128)(2,1)} %bitcast.51) | data formatting | bytes 16777216 | tf_op jit(solution)/shard_map/all_to_all | solution.py:55
  478.1 15.8 %copy.35 = bf16[512,32,2,128]{0,1,2,3:T(8,128)(2,1)} copy(bf16[512,32,2,128]{3,1,2,0:T(8,128)(2,1)} %bitcast.55) | data formatting | bytes 16777216 | tf_op jit(solution)/shard_map/all_to_all | solution.py:55
  493.9 103.5 %all_to_all.37 = bf16[512,32,2,128]{0,1,2,3:T(8,128)(2,1)} all-to-all(bf16[512,32,2,128]{0,1,2,3:T(8,128)(2,1)} %copy.35), channel_id=1, replica_groups=mesh['station'=8,'tm'=16] {'tm'}, dimensions={3} | all-to-all | bytes 16777216 | tf_op jit(solution)/shard_map/all_to_all | solution.py:54
  597.5 12.7 %copy.37 = bf16[512,16,32,2,8]{0,4,3,2,1:T(8,128)(2,1)} copy(bf16[512,16,32,2,8]{0,2,3,4,1:T(8,128)(2,1)} %bitcast.58) | data formatting | bytes 16777216 | tf_op jit(solution)/shard_map/all_to_all | solution.py:54
  610.2 15.7 %copy.41 = bf16[8,512,2,512]{3,2,1,0:T(2,128)(2,1)} copy(bf16[8,512,2,512]{1,0,2,3:T(8,128)(2,1)} %bitcast.47) | data formatting | bytes 16777216 | tf_op jit(solution)/shard_map/transpose | solution.py:63
  625.8 11.4 %copy.39 = bf16[8,512,2,512]{1,3,2,0:T(8,128)(2,1)} copy(bf16[8,512,2,512]{1,0,2,3:T(8,128)(2,1)} %bitcast.48) | data formatting | bytes 16777216 | tf_op jit(solution)/shard_map/transpose | solution.py:63
  637.2 13.9 %copy.38 = bf16[512,512,2,8]{1,0,3,2:T(8,128)(2,1)} copy(bf16[512,512,2,8]{0,3,2,1:T(8,128)(2,1)} %bitcast.49) | data formatting | bytes 16777216 | tf_op jit(solution)/shard_map/all_to_all | solution.py:54
  657.0 11.5 %copy.40 = bf16[8,1,512,1024]{3,2,1,0:T(8,128)(2,1)} copy(bf16[8,1,512,1024]{2,3,0,1:T(8,128)(2,1)} %bitcast.56) | data formatting | bytes 16777216 | tf_op jit(solution)/shard_map/stack;reshape | solution.py:29
  668.5 14.3 %reshape.29 = bf16[8,512,1024,1]{2,1,0,3:T(8,128)(2,1)} reshape(bf16[8,512,2,512]{3,2,1,0:T(2,128)(2,1)} %copy.41) | data formatting | bytes 16777216 | tf_op jit(solution)/shard_map/reshape | solution.py:64
  682.9 8.0 %maximum_bitcast_fusion = bf16[8,1,512,1024]{3,2,1,0:T(8,128)(2,1)} fusion(bf16[8,512,512]{2,1,0:T(8,128)(2,1)} %get-tuple-element.6, bf16[8,512,512]{2,1,0:T(8,128)(2,1)} %get-tuple-element.5), kind=kLoop, calls=%fused_computation.14 | loop fusion | flops 16777216 | bytes 16777216 | tf_op jit(solution)/shard_map/stack | solution.py:29
  690.8 17.0 %multiply_bitcast_fusion = f32[8,2,512,512]{2,3,1,0:T(8,128)} fusion(bf16[8,1,512,1024]{3,2,1,0:T(8,128)(2,1)} %maximum_bitcast_fusion, bf16[8,1,512,1024]{3,2,1,0:T(8,128)(2,1)} %copy.40, bf16[8,512,1024,1]{2,1,0,3:T(8,128)(2,1)} %reshape.29), kind=kOutput, calls=%fused_computation.4 | convolution fusion | flops 8602517504 | bytes 41943040 | tf_op jit(solution)/shard_map/cit,crjt->crij/dot_general | solution.py:30
  707.8 17.5 %copy.42 = f32[8,2,512,512]{3,2,1,0:T(8,128)} copy(f32[8,2,512,512]{2,3,1,0:T(8,128)} %multiply_bitcast_fusion) | data formatting | bytes 33554432 | tf_op jit(solution)/shard_map/mul | solution.py:67
  (12 shorter events, 26.5 us)
Async XLA Ops:
  0.0 100.7 %slice-start = ((s8[8388608]{0:T(1024)(128)(4,1)}), s8[4194304]{0:T(1024)(128)(4,1)S(1)}, s32[]{:S(2)}) async-start(s8[8388608]{0:T(1024)(128)(4,1)} %bitcast.52), calls=%async_computation.2 | async-start | bytes 8388608
  6.9 87.1 %collective-permute-start = (bf16[64,15,2,1024]{3,2,1,0:T(2,128)(2,1)}, bf16[64,15,2,1024]{3,2,1,0:T(2,128)(2,1)}, u32[]{:S(2)}, u32[]{:S(2)}) collective-permute-start(bf16[64,15,2,1024]{3,2,1,0:T(2,128)(2,1)} %slice.104), channel_id=1, source_target_pairs={{0,1},{1,2},{2,3},{3,4},{4,5},{5,6},{6,7},{7,8},{8,9},{9,10},{10,1... | collective-permute-start | bytes 11796488 | tf_op jit(solution)/shard_map/ppermute | solution.py:12
  30.3 70.5 %slice-start.1 = ((s8[8388608]{0:T(1024)(128)(4,1)}), s8[4194304]{0:T(1024)(128)(4,1)S(1)}, s32[]{:S(2)}) async-start(s8[8388608]{0:T(1024)(128)(4,1)} %bitcast.52), calls=%async_computation.3 | async-start | bytes 8388608
  236.9 10.5 %copy-start = (bf16[1024,1024]{1,0:T(8,128)(2,1)S(1)}, bf16[1024,1024]{1,0:T(8,128)(2,1)}, u32[]{:S(2)}) copy-start(bf16[1024,1024]{1,0:T(8,128)(2,1)} %fusion.25) | copy-start | bytes 6291460
where the time goes:
time: 735 us; the launch traced here: 726 us
  local copies, waits for them, and re-layouts  249 us (34%)
  blocking collectives  204 us (28%)
  other arithmetic  178 us (24%)
  waiting for transfers between devices  45.8 us (6%)
  matrix products  43.2 us (6%)
    convert_element_type x1, other arithmetic, per_device(): filtered = total.astype(jnp.bfloat16).reshape(-1, 2 * nfft)  129 us
    all_to_all x1, blocking collectives, per_device(): lax.all_to_all(lax.all_to_all(spectra, 'station', split_axis=3, concat_ax...  104 us
    all_to_all x1, blocking collectives, per_device(): lax.all_to_all(spectra, 'station', split_axis=3, concat_axis=0, tiled=True)  101 us
    unnamed x10, local copies, waits for them, and re-layouts  50.6 us
    ppermute x1, waiting for transfers between devices, passed_along(): lax.ppermute(value, axis, [(source, source + steps) for source in range(l...  45.8 us
    all_to_all x2, local copies, waits for them, and re-layouts, per_device(): lax.all_to_all(spectra, 'station', split_axis=3, concat_axis=0, tiled=True)  43.6 us
    reshape x2, local copies, waits for them, and re-layouts, per_device(): spectra = spectra.reshape(inputs_here, frames, 2, nfft)  42.8 us
    another operation x2, other arithmetic  34.5 us
  transfers between devices with their start and end apart: 1, of which 1 were waited for; matrix products, arithmetic and copies ran while one was open for 5% of the time, Pallas kernels for 0%

commit v1 on v0

v1 whole, which is shorter than its diff:
```python
import functools
import math

import jax
import jax.numpy as jnp
import ml_dtypes
import numpy as np
from jax import lax
from jax.experimental import pallas as pl
from jax.experimental.pallas import tpu as pltpu
from jax.sharding import PartitionSpec as P

AXES = ("station", "tm")
BEFORE = 8
INPUT_BLOCK = 16
PITCH = 24
EDGE_STEPS = 4
VMEM_BYTES = 60 * 1024 * 1024


def transform_rows(nfft):
    channel = np.arange(nfft, dtype=np.int64).reshape(nfft // 4, 4).T
    product = channel[:, :, None] * np.arange(nfft // 4, dtype=np.int64) % nfft
    angle = (np.float32(2.0 * math.pi / nfft) * product.astype(np.float32)).astype(np.float32)
    scale = np.float32(math.sqrt(nfft))
    parts = np.concatenate([np.cos(angle) / scale, np.sin(angle) / scale], axis=2)
    return parts.astype(ml_dtypes.bfloat16)


def filter_group(outputs, first, last, get, taps_ref, keep, wrap):
    tap_count = taps_ref.shape[0]
    own = [None] * len(outputs)
    for e in range(first, last):
        if wrap is not None and e == wrap:
            own = [a if f < wrap else a * keep for f, a in zip(outputs, own)]
        value = get(e).astype(jnp.float32)
        for n, f in enumerate(outputs):
            if 0 <= f - e < tap_count:
                term = taps_ref[f - e] * value
                own[n] = term if own[n] is None else own[n] + term
    return own


def channelize_body(groups, wrap, own_first, own_count, *refs):
    if wrap is None:
        taps_ref, table_ref, own_ref, out_ref, filtered, data, turned = refs
        keep = None
        before_ref = after_ref = None
    else:
        (keep_ref, taps_ref, table_ref, own_ref, before_ref, after_ref, out_ref, filtered, data, turned) = refs
        keep = keep_ref[0]
    step = pl.program_id(0)
    rows = INPUT_BLOCK

    def filter_input(i, _):
        def get(e):
            if e < own_first:
                return before_ref[i, e]
            if e < own_first + own_count:
                return own_ref[i, e - own_first]
            return after_ref[i, e - own_first - own_count]

        done = 0
        for outputs in groups:
            first = outputs[0] - (taps_ref.shape[0] - 1)
            values = filter_group(outputs, first, outputs[-1] + 1, get, taps_ref, keep, wrap)
            for n, value in enumerate(values):
                filtered[done + n, pl.ds(pl.multiple_of(i * PITCH, 8), 16), :] = value
            done += len(outputs)
        return 0

    lax.fori_loop(0, rows, filter_input, 0)

    def place(f, _):
        at = pl.ds(pl.multiple_of(step * rows, rows), rows)

        def sample(j):
            return [filtered[f, pl.ds(2 * j + part, rows, stride=PITCH), :] for part in range(2)]

        for q in range(2):
            z = [sample(q + 2 * m) for m in range(4)]
            even = [[a + b for a, b in zip(z[m], z[m + 2])] for m in range(2)]
            odd = [[a - b for a, b in zip(z[m], z[m + 2])] for m in range(2)]
            turned_odd = [odd[1][1], -odd[1][0]]
            folded = [
                [a + b for a, b in zip(even[0], even[1])],
                [a + b for a, b in zip(odd[0], turned_odd)],
                [a - b for a, b in zip(even[0], even[1])],
                [a - b for a, b in zip(odd[0], turned_odd)],
            ]
            low, high = pl.ds(q * 128, 128), pl.ds(256 + q * 128, 128)
            for p, (re, im) in enumerate(folded):
                re, im = re.astype(jnp.bfloat16), im.astype(jnp.bfloat16)
                data[p, f, 0, at, low] = re
                data[p, f, 0, at, high] = im
                data[p, f, 1, at, low] = im
                data[p, f, 1, at, high] = -re
        return 0

    lax.fori_loop(0, 16, place, 0)

    @pl.when(step == pl.num_programs(0) - 1)
    def _():
        def transform(n, _):
            for p in range(4):
                pair = data[p, pl.ds(2 * n, 2)].reshape(256, 512)
                result = lax.dot_general(
                    table_ref[p], pair, (((1,), (1,)), ((), ())), preferred_element_type=jnp.float32
                )
                turned[pl.ds(16 * p + 2 * n, 256, stride=64), :] = result[:, :128]
                turned[pl.ds(16 * p + 2 * n + 1, 256, stride=64), :] = result[:, 128:]
            return 0

        lax.fori_loop(0, 8, transform, 0)

        def write(d, _):
            block = turned[pl.ds(pl.multiple_of(d * 256, 256), 256), :]
            out_ref[pl.ds(2 * d, 2)] = block.reshape(2, 8, 16, 128).astype(jnp.bfloat16)
            return 0

        lax.fori_loop(0, 64, write, 0)


def channelize(groups, wrap, own_first, keep, taps, table, own, before, after, devices):
    inputs, own_count = own.shape[0], own.shape[1]
    whole = pl.BlockSpec(memory_space=pltpu.VMEM)

    def per_input(array):
        return pl.BlockSpec((INPUT_BLOCK,) + array.shape[1:], lambda s: (s, 0, 0, 0))

    operands, specs = [taps, table, own], [whole, whole, per_input(own)]
    if wrap is not None:
        operands = [keep] + operands + [before, after]
        specs = [pl.BlockSpec(memory_space=pltpu.SMEM)] + specs + [per_input(before), per_input(after)]
    return pl.pallas_call(
        functools.partial(channelize_body, groups, wrap, own_first, own_count),
        grid=(inputs // INPUT_BLOCK,),
        in_specs=specs,
        out_specs=whole,
        out_shape=jax.ShapeDtypeStruct((devices, 8, 16, 128), jnp.bfloat16),
        scratch_shapes=[
            pltpu.VMEM((16, INPUT_BLOCK * PITCH, 128), jnp.float32),
            pltpu.VMEM((4, 16, 2, 64, 512), jnp.bfloat16),
            pltpu.VMEM((1024 * 16, 128), jnp.float32),
        ],
        compiler_params=pltpu.CompilerParams(vmem_limit_bytes=VMEM_BYTES),
        cost_estimate=pl.CostEstimate(
            flops=64 * 1024 * 2048 * 2048, bytes_accessed=17 * 1024 * 1024, transcendentals=0
        ),
    )(*operands)


def edges_body(first_ref, last_ref, head_ref, tail_ref):
    head_ref[...] = first_ref[:, : head_ref.shape[1]]
    tail_ref[...] = last_ref[...]


def edges(own, head):
    inputs, frames = own.shape[:2]
    rows = inputs // EDGE_STEPS
    shapes = [(inputs, count) + own.shape[2:] for count in (head, BEFORE)]
    last = frames // BEFORE - 1
    return pl.pallas_call(
        edges_body,
        grid=(EDGE_STEPS,),
        in_specs=[
            pl.BlockSpec((rows, BEFORE) + own.shape[2:], lambda s: (s, 0, 0, 0)),
            pl.BlockSpec((rows, BEFORE) + own.shape[2:], lambda s: (s, last, 0, 0)),
        ],
        out_specs=[pl.BlockSpec((rows,) + shape[1:], lambda s: (s, 0, 0, 0)) for shape in shapes],
        out_shape=[jax.ShapeDtypeStruct(shape, own.dtype) for shape in shapes],
        compiler_params=pltpu.CompilerParams(vmem_limit_bytes=VMEM_BYTES),
    )(own, own)


def unpack_pair(low, high):
    real = jnp.concatenate([low[:, :64], high[:, :64]], axis=1)
    return real, jnp.concatenate([low[:, 64:], high[:, 64:]], axis=1)


def unpack_into(ref, store):
    for p in range(4):
        low = ref[pl.ds(32 * p, 16), 0].reshape(256, 128)
        high = ref[pl.ds(32 * p + 16, 16), 0].reshape(256, 128)
        store(pl.ds(128 * p, 128), *unpack_pair(low, high))


def received(spectra):
    return pl.BlockSpec((spectra.shape[0], 1, 16, 128), lambda c: (0, c, 0, 0))


def unpack_body(ref, out_ref):
    def store(at, real, imag):
        out_ref[0, 0, :, at] = real
        out_ref[0, 1, :, at] = imag

    unpack_into(ref, store)


def unpack(spectra):
    channels = spectra.shape[1]
    return pl.pallas_call(
        unpack_body,
        grid=(channels,),
        in_specs=[received(spectra)],
        out_specs=pl.BlockSpec((1, 2, 256, 512), lambda c: (c, 0, 0, 0)),
        out_shape=jax.ShapeDtypeStruct((channels, 2, 256, 512), jnp.bfloat16),
        compiler_params=pltpu.CompilerParams(vmem_limit_bytes=VMEM_BYTES),
        cost_estimate=pl.CostEstimate(
            flops=64 * 1024 * 2048 * 2048, bytes_accessed=9 * 1024 * 1024, transcendentals=0
        ),
    )(spectra)


def correlate_body(scale, ready_ref, ref, out_ref, real, imag):
    real[pl.ds(0, 256), :] = ready_ref[0, 0]
    imag[pl.ds(0, 256), :] = ready_ref[0, 1]

    def store(at, re, im):
        real[pl.ds(256, 256), at] = re
        imag[pl.ds(256, 256), at] = im

    unpack_into(ref, store)
    r, i = real[...], imag[...]
    rt, it = r.T, i.T

    def block(left, right, m, n):
        return jnp.dot(
            left[256 * m : 256 * m + 256], right[:, 256 * n : 256 * n + 256], preferred_element_type=jnp.float32
        )

    for m, n in ((0, 0), (0, 1), (1, 1)):
        rows, columns = pl.ds(256 * m, 256), pl.ds(256 * n, 256)
        value = (block(rt, r, m, n) + block(it, i, m, n)) * scale
        cross = block(it, r, m, n) * scale
        out_ref[0, 0, rows, columns] = value
        if m == n:
            out_ref[0, 1, rows, columns] = cross - cross.T
        else:
            cross = cross - block(rt, i, m, n) * scale
            out_ref[0, 0, columns, rows] = value.T
            out_ref[0, 1, rows, columns] = cross
            out_ref[0, 1, columns, rows] = -cross.T


def correlate(first, second, frames):
    channels = second.shape[1]
    return pl.pallas_call(
        functools.partial(correlate_body, 1.0 / frames),
        grid=(channels,),
        in_specs=[pl.BlockSpec((1, 2, 256, 512), lambda c: (c, 0, 0, 0)), received(second)],
        out_specs=pl.BlockSpec((1, 2, 512, 512), lambda c: (c, 0, 0, 0)),
        out_shape=jax.ShapeDtypeStruct((channels, 2, 512, 512), jnp.float32),
        scratch_shapes=[pltpu.VMEM((512, 512), jnp.bfloat16)] * 2,
        compiler_params=pltpu.CompilerParams(vmem_limit_bytes=VMEM_BYTES),
        cost_estimate=pl.CostEstimate(
            flops=16 * 512 * 512 * 1024, bytes_accessed=25 * 1024 * 1024, transcendentals=0
        ),
    )(first, second)


def per_device(voltages, taps):
    inputs, frames, _, nfft = voltages.shape
    tap_count = taps.shape[0]
    n_tm = lax.axis_size("tm")
    devices = n_tm * lax.axis_size("station")
    after_count = tap_count - 1 - BEFORE

    def blocked(a):
        return a.reshape(a.shape[0], a.shape[1], 2, 8, 128).transpose(0, 1, 3, 2, 4).reshape(a.shape[0], a.shape[1], 16, 128)

    own = blocked(voltages)
    up = [(d, d + 1) for d in range(n_tm - 1)]
    down = [(d, (d - 1) % n_tm) for d in range(n_tm)]
    head, tail = edges(own, after_count)
    before = lax.ppermute(tail, "tm", up)
    after = lax.ppermute(head, "tm", down)
    taps_rows = jnp.repeat(taps.reshape(tap_count, 8, 1, 128), 2, axis=2).reshape(tap_count, 16, 128)
    table = jnp.asarray(transform_rows(nfft))
    keep = (lax.axis_index("tm") < n_tm - 1).astype(jnp.float32).reshape(1)

    inner = [tuple(range(15, 23)), tuple(range(23, 31))]
    outer = [tuple(range(15, 23)), tuple(range(39, 47))]
    first = channelize(inner, None, 0, None, taps_rows, table, own, None, None, devices)
    first, after = lax.optimization_barrier((first, after))
    second = channelize(outer, BEFORE + frames, BEFORE, keep, taps_rows, table, own, before, after, devices)
    first = lax.all_to_all(first, AXES, 0, 0, tiled=True)
    second = lax.all_to_all(second, AXES, 0, 0, tiled=True)
    return correlate(unpack(first), second, n_tm * frames)


def solution(mesh):
    return jax.shard_map(
        per_device,
        mesh=mesh,
        in_specs=(P("station", "tm", None, None), P()),
        out_specs=P(("station", "tm"), None, None, None),
        check_vma=False,
    )
```

time: 735 us -> 185 us (0.25); the launches traced: 726 us -> 184 us
  local copies, waits for them, and re-layouts: 249 us -> 0.73 us
  blocking collectives: 204 us -> 0 us
  other arithmetic: 178 us -> 0 us
  Pallas kernels: 0 us -> 74.5 us
  matrix products: 43.2 us -> 0 us
  waiting for transfers between devices: 45.8 us -> 83.9 us
  starting transfers between devices: 5.56 us -> 25.3 us
    all_to_all x2 -> x0, blocking collectives: 204 us -> none  [the longest x1 104 us: per_device(): lax.all_to_all(lax.all_to_all(spectra, 'station', split_axis=3, concat_ax...]
    convert_element_type x1 -> x0, other arithmetic: 129 us -> none  [per_device(): filtered = total.astype(jnp.bfloat16).reshape(-1, 2 * nfft)]
    pallas_call x0 -> x5, Pallas kernels: none -> 74.5 us  [the longest x2 48.3 us: channelize(): pl.pallas_call(functools.partial(channelize_body, groups, wrap, own_first...]
    all_to_all x0 -> x2, waiting for transfers between devices: none -> 72 us  [the longest x1 44.6 us: per_device(): second = lax.all_to_all(second, AXES, 0, 0, tiled=True)]
    all_to_all x4 -> x0, local copies, waits for them, and re-layouts: 70.1 us -> none  [the longest x2 43.6 us: per_device(): lax.all_to_all(spectra, 'station', split_axis=3, concat_axis=0, tiled=True)]
    reshape x3 -> x0, local copies, waits for them, and re-layouts: 57.1 us -> none  [the longest x2 42.8 us: per_device(): spectra = spectra.reshape(inputs_here, frames, 2, nfft)]
    unnamed x10 -> x3, local copies, waits for them, and re-layouts: 50.6 us -> 0.02 us
    dot_general x2 -> x0, matrix products: 43.2 us -> none  [the longest x1 26.2 us: per_device(): jnp.dot(filtered, table, preferred_element_type=jnp.float32)]
  transfers between devices with their start and end apart: 1 -> 4, of which waited for: 1 -> 3; matrix products, arithmetic and copies ran while one was open for 5% -> 0% of each run, Pallas kernels for 0% -> 30%
where the time goes in v1:
time: 185 us; the launch traced here: 184 us
  waiting for transfers between devices  83.9 us (45%)
  Pallas kernels  74.5 us (40%)
  starting transfers between devices  25.3 us (14%)
    pallas_call x2, Pallas kernels, channelize(): pl.pallas_call(functools.partial(channelize_body, groups, wrap, own_first...  48.3 us
    all_to_all x1, waiting for transfers between devices, per_device(): second = lax.all_to_all(second, AXES, 0, 0, tiled=True)  44.6 us
    all_to_all x1, waiting for transfers between devices, per_device(): first = lax.all_to_all(first, AXES, 0, 0, tiled=True)  27.4 us
    pallas_call x1, Pallas kernels, correlate(): pl.pallas_call(functools.partial(correlate_body, 1.0 / frames), grid=(cha...  14.3 us
    ppermute x1, waiting for transfers between devices, per_device(): after = lax.ppermute(head, 'tm', down)  11.9 us
    all_to_all x1, starting transfers between devices, per_device(): first = lax.all_to_all(first, AXES, 0, 0, tiled=True)  11.2 us
    pallas_call x1, Pallas kernels, unpack(): pl.pallas_call(unpack_body, grid=(channels,), in_specs=[received(spectra)...  7.33 us
    ppermute x1, starting transfers between devices, per_device(): after = lax.ppermute(head, 'tm', down)  6.21 us
  transfers between devices with their start and end apart: 4, of which 3 were waited for; matrix products, arithmetic and copies ran while one was open for 0% of the time, Pallas kernels for 30%

profile of v1, /device:TPU:7, one launch (start us, length us, event | category | flops | bytes accessed | tf_op | source)
XLA Modules:
  0.0 184.4 jit_solution(15385579435863275424)
XLA Ops:
  0.0 0.0 copy-start
  0.0 4.6 %shard_map.38 = (bf16[64,7,16,128]{3,2,1,0:T(8,128)(2,1)}, bf16[64,8,16,128]{3,2,1,0:T(8,128)(2,1)}) custom-call(bf16[64,32,16,128]{3,2,1,0:T(8,128)(2,1)} %bitcast.9, bf16[64,32,16,128]{3,2,1,0:T(8,128)(2,1)} %bitcast.10), custom_call_target="tpu_custom_call" | custom-call | tf_op jit(solution)/shard_map/pallas_call | solution.py:163
  4.6 6.2 %collective-permute-start = (bf16[64,7,16,128]{3,2,1,0:T(8,128)(2,1)}, bf16[64,7,16,128]{3,2,1,0:T(8,128)(2,1)}, u32[]{:S(2)}, u32[]{:S(2)}) collective-permute-start(bf16[64,7,16,128]{3,2,1,0:T(8,128)(2,1)} %get-tuple-element.9), channel_id=1, source_target_pairs={{0,15},{1,0},{2,1},{3,2},{4,3},{5,4},{6,5},{7,6},{8,7},{9,8},{10,9... | collective-permute-start | bytes 5505032 | tf_op jit(solution)/shard_map/ppermute | solution.py:277
  10.8 2.6 %collective-permute-start.1 = (bf16[64,8,16,128]{3,2,1,0:T(8,128)(2,1)}, bf16[64,8,16,128]{3,2,1,0:T(8,128)(2,1)}, u32[]{:S(2)}, u32[]{:S(2)}) collective-permute-start(bf16[64,8,16,128]{3,2,1,0:T(8,128)(2,1)} %get-tuple-element.11), channel_id=1, source_target_pairs={{0,1},{1,2},{2,3},{3,4},{4,5},{5,6},{6,7},{7,8},{8,9},{9,10},{10,1... | collective-permute-start | bytes 6291464 | tf_op jit(solution)/shard_map/ppermute | solution.py:276
  13.5 0.0 copy-done
  13.5 0.7 broadcast_in_dim.3
  14.2 23.8 %shard_map.37 = bf16[128,8,16,128]{3,2,1,0:T(8,128)(2,1)} custom-call(f32[16,16,128]{2,1,0:T(8,128)} %bitcast.14, bf16[4,256,512]{2,1,0:T(8,128)(2,1)} %constant.8.clone.refs_1_.refs_2_, bf16[64,32,16,128]{3,2,1,0:T(8,128)(2,1)} %bitcast.11), custom_call_target="tpu_custom_call" | custom-call | flops 274877906944 | bytes 17825792 | tf_op jit(solution)/shard_map/pallas_call | solution.py:135
  38.0 11.9 %collective-permute-done.refs_5_ = bf16[64,7,16,128]{3,2,1,0:T(8,128)(2,1)} collective-permute-done((bf16[64,7,16,128]{3,2,1,0:T(8,128)(2,1)}, bf16[64,7,16,128]{3,2,1,0:T(8,128)(2,1)}, u32[]{:S(2)}, u32[]{:S(2)}) %collective-permute-start) | collective-permute-done | bytes 1835040 | tf_op jit(solution)/shard_map/ppermute | solution.py:277
  49.8 11.2 %all-to-all-start = ((bf16[128,8,16,128]{3,2,1,0:T(8,128)(2,1)}), bf16[128,8,16,128]{3,2,1,0:T(8,128)(2,1)}, u32[]{:S(2)}, u32[]{:S(2)}) async-start(bf16[128,8,16,128]{3,2,1,0:T(8,128)(2,1)} %shard_map.37), calls=%async_computation | async-start | bytes 8388608 | tf_op jit(solution)/shard_map/all_to_all | solution.py:287
  61.1 0.0 collective-permute-done.1.refs_4_
  61.1 24.5 %shard_map.40 = bf16[128,8,16,128]{3,2,1,0:T(8,128)(2,1)} custom-call(f32[1]{0:T(128)} %bitcast.6.refs_0_, f32[16,16,128]{2,1,0:T(8,128)} %bitcast.15, bf16[4,256,512]{2,1,0:T(8,128)(2,1)} %constant.8.clone.refs_1_.refs_2_, bf16[64,32,16,128]{3,2,1,0:T(8,128)(2,1)} %bitcast.12, bf16[64,8,16,128]{3,2,1,0:T(8,128)(2,1)} %collective-permute-done.1.refs_4_, ...), custom_call_target="tpu_custom_call" | custom-call | flops 274877906944 | bytes 17825792 | tf_op jit(solution)/shard_map/pallas_call | solution.py:135
  85.6 27.4 %all-to-all-done.ref = bf16[128,8,16,128]{3,2,1,0:T(8,128)(2,1)} async-done(((bf16[128,8,16,128]{3,2,1,0:T(8,128)(2,1)}), bf16[128,8,16,128]{3,2,1,0:T(8,128)(2,1)}, u32[]{:S(2)}, u32[]{:S(2)}) %all-to-all-start) | async-done | bytes 4194336 | tf_op jit(solution)/shard_map/all_to_all | solution.py:287
  113.0 5.2 %all-to-all-start.1 = ((bf16[128,8,16,128]{3,2,1,0:T(8,128)(2,1)}), bf16[128,8,16,128]{3,2,1,0:T(8,128)(2,1)}, u32[]{:S(2)}, u32[]{:S(2)}) async-start(bf16[128,8,16,128]{3,2,1,0:T(8,128)(2,1)} %shard_map.40), calls=%async_computation.1 | async-start | bytes 8388608 | tf_op jit(solution)/shard_map/all_to_all | solution.py:288
  118.2 7.3 %shard_map.39.ready_ref = bf16[8,2,256,512]{3,2,1,0:T(8,128)(2,1)} custom-call(bf16[128,8,16,128]{3,2,1,0:T(8,128)(2,1)} %all-to-all-done.ref), custom_call_target="tpu_custom_call" | custom-call | flops 274877906944 | bytes 9437184 | tf_op jit(solution)/shard_map/pallas_call | solution.py:202
  125.5 44.6 %all-to-all-done.1.ref = bf16[128,8,16,128]{3,2,1,0:T(8,128)(2,1)} async-done(((bf16[128,8,16,128]{3,2,1,0:T(8,128)(2,1)}), bf16[128,8,16,128]{3,2,1,0:T(8,128)(2,1)}, u32[]{:S(2)}, u32[]{:S(2)}) %all-to-all-start.1) | async-done | bytes 4194336 | tf_op jit(solution)/shard_map/all_to_all | solution.py:288
  170.1 14.3 %shard_map.41 = f32[8,2,512,512]{3,2,1,0:T(8,128)} custom-call(bf16[8,2,256,512]{3,2,1,0:T(8,128)(2,1)} %shard_map.39.ready_ref, bf16[128,8,16,128]{3,2,1,0:T(8,128)(2,1)} %all-to-all-done.1.ref), custom_call_target="tpu_custom_call" | custom-call | flops 4294967296 | bytes 26214400 | tf_op jit(solution)/shard_map/pallas_call | solution.py:248
  (1 shorter events, 0.0 us)
Async XLA Ops:
  0.0 13.5 %copy-start = (f32[16,1024]{1,0:T(8,128)S(1)}, f32[16,1024]{1,0:T(8,128)}, u32[]{:S(2)}) copy-start(f32[16,1024]{1,0:T(8,128)} %param.4) | copy-start | bytes 196612
  4.6 45.2 %collective-permute-start = (bf16[64,7,16,128]{3,2,1,0:T(8,128)(2,1)}, bf16[64,7,16,128]{3,2,1,0:T(8,128)(2,1)}, u32[]{:S(2)}, u32[]{:S(2)}) collective-permute-start(bf16[64,7,16,128]{3,2,1,0:T(8,128)(2,1)} %get-tuple-element.9), channel_id=1, source_target_pairs={{0,15},{1,0},{2,1},{3,2},{4,3},{5,4},{6,5},{7,6},{8,7},{9,8},{10,9... | collective-permute-start | bytes 5505032 | tf_op jit(solution)/shard_map/ppermute | solution.py:277
  10.8 50.3 %collective-permute-start.1 = (bf16[64,8,16,128]{3,2,1,0:T(8,128)(2,1)}, bf16[64,8,16,128]{3,2,1,0:T(8,128)(2,1)}, u32[]{:S(2)}, u32[]{:S(2)}) collective-permute-start(bf16[64,8,16,128]{3,2,1,0:T(8,128)(2,1)} %get-tuple-element.11), channel_id=1, source_target_pairs={{0,1},{1,2},{2,3},{3,4},{4,5},{5,6},{6,7},{7,8},{8,9},{9,10},{10,1... | collective-permute-start | bytes 6291464 | tf_op jit(solution)/shard_map/ppermute | solution.py:276
  49.8 63.2 %all-to-all-start = ((bf16[128,8,16,128]{3,2,1,0:T(8,128)(2,1)}), bf16[128,8,16,128]{3,2,1,0:T(8,128)(2,1)}, u32[]{:S(2)}, u32[]{:S(2)}) async-start(bf16[128,8,16,128]{3,2,1,0:T(8,128)(2,1)} %shard_map.37), calls=%async_computation | async-start | bytes 8388608 | tf_op jit(solution)/shard_map/all_to_all | solution.py:287
  113.0 57.1 %all-to-all-start.1 = ((bf16[128,8,16,128]{3,2,1,0:T(8,128)(2,1)}), bf16[128,8,16,128]{3,2,1,0:T(8,128)(2,1)}, u32[]{:S(2)}, u32[]{:S(2)}) async-start(bf16[128,8,16,128]{3,2,1,0:T(8,128)(2,1)} %shard_map.40), calls=%async_computation.1 | async-start | bytes 8388608 | tf_op jit(solution)/shard_map/all_to_all | solution.py:288

commit v2 on v1

--- a/solution.py
+++ b/solution.py
@@ -14,7 +14,7 @@
 BEFORE = 8
 INPUT_BLOCK = 16
 PITCH = 24
-EDGE_STEPS = 4
+EDGE_STEPS = 2
 VMEM_BYTES = 60 * 1024 * 1024
 
 
@@ -282,7 +282,7 @@
     inner = [tuple(range(15, 23)), tuple(range(23, 31))]
     outer = [tuple(range(15, 23)), tuple(range(39, 47))]
     first = channelize(inner, None, 0, None, taps_rows, table, own, None, None, devices)
-    first, after = lax.optimization_barrier((first, after))
+    first, before = lax.optimization_barrier((first, before))
     second = channelize(outer, BEFORE + frames, BEFORE, keep, taps_rows, table, own, before, after, devices)
     first = lax.all_to_all(first, AXES, 0, 0, tiled=True)
     second = lax.all_to_all(second, AXES, 0, 0, tiled=True)

time: 185 us -> 191 us (1.032)
  waiting for transfers between devices: 83.9 us -> 90.8 us
    ppermute x1, waiting for transfers between devices: 0.01 us -> 18.8 us  [per_device(): before = lax.ppermute(tail, 'tm', up)]
    ppermute x1, waiting for transfers between devices: 11.9 us -> 0.01 us  [per_device(): after = lax.ppermute(head, 'tm', down)]
  transfers between devices with their start and end apart: 4 -> 4, of which waited for: 3 -> 3; matrix products, arithmetic and copies ran while one was open for 0% -> 0% of each run, Pallas kernels for 30% -> 29%
where the time goes in v2:
time: 191 us; the launch traced here: 190 us
  waiting for transfers between devices  90.8 us (48%)
  Pallas kernels  73.5 us (38%)
  starting transfers between devices  24.8 us (13%)
    pallas_call x2, Pallas kernels, channelize(): pl.pallas_call(functools.partial(channelize_body, groups, wrap, own_first...  48.3 us
    all_to_all x1, waiting for transfers between devices, per_device(): second = lax.all_to_all(second, AXES, 0, 0, tiled=True)  44.6 us
    all_to_all x1, waiting for transfers between devices, per_device(): first = lax.all_to_all(first, AXES, 0, 0, tiled=True)  27.4 us
    ppermute x1, waiting for transfers between devices, per_device(): before = lax.ppermute(tail, 'tm', up)  18.8 us
    pallas_call x1, Pallas kernels, correlate(): pl.pallas_call(functools.partial(correlate_body, 1.0 / frames), grid=(cha...  14.3 us
    all_to_all x1, starting transfers between devices, per_device(): first = lax.all_to_all(first, AXES, 0, 0, tiled=True)  10.8 us
    pallas_call x1, Pallas kernels, unpack(): pl.pallas_call(unpack_body, grid=(channels,), in_specs=[received(spectra)...  7.33 us
    ppermute x1, starting transfers between devices, per_device(): after = lax.ppermute(head, 'tm', down)  6.21 us
  transfers between devices with their start and end apart: 4, of which 3 were waited for; matrix products, arithmetic and copies ran while one was open for 0% of the time, Pallas kernels for 29%

profile of v2, /device:TPU:7, one launch (start us, length us, event | category | flops | bytes accessed | tf_op | source)
XLA Modules:
  0.0 189.9 jit_solution(1338247613287679379)
XLA Ops:
  0.0 0.0 copy-start
  0.0 3.7 %shard_map.38 = (bf16[64,7,16,128]{3,2,1,0:T(8,128)(2,1)}, bf16[64,8,16,128]{3,2,1,0:T(8,128)(2,1)}) custom-call(bf16[64,32,16,128]{3,2,1,0:T(8,128)(2,1)} %bitcast.9, bf16[64,32,16,128]{3,2,1,0:T(8,128)(2,1)} %bitcast.10), custom_call_target="tpu_custom_call" | custom-call | tf_op jit(solution)/shard_map/pallas_call | solution.py:163
  3.7 6.2 %collective-permute-start.1 = (bf16[64,7,16,128]{3,2,1,0:T(8,128)(2,1)}, bf16[64,7,16,128]{3,2,1,0:T(8,128)(2,1)}, u32[]{:S(2)}, u32[]{:S(2)}) collective-permute-start(bf16[64,7,16,128]{3,2,1,0:T(8,128)(2,1)} %get-tuple-element.12), channel_id=1, source_target_pairs={{0,15},{1,0},{2,1},{3,2},{4,3},{5,4},{6,5},{7,6},{8,7},{9,8},{10,9... | collective-permute-start | bytes 5505032 | tf_op jit(solution)/shard_map/ppermute | solution.py:277
  9.9 2.6 %collective-permute-start = (bf16[64,8,16,128]{3,2,1,0:T(8,128)(2,1)}, bf16[64,8,16,128]{3,2,1,0:T(8,128)(2,1)}, u32[]{:S(2)}, u32[]{:S(2)}) collective-permute-start(bf16[64,8,16,128]{3,2,1,0:T(8,128)(2,1)} %get-tuple-element.9), channel_id=1, source_target_pairs={{0,1},{1,2},{2,3},{3,4},{4,5},{5,6},{6,7},{7,8},{8,9},{9,10},{10,1... | collective-permute-start | bytes 6291464 | tf_op jit(solution)/shard_map/ppermute | solution.py:276
  12.5 0.0 copy-done
  12.5 0.7 broadcast_in_dim.3
  13.2 23.7 %shard_map.37 = bf16[128,8,16,128]{3,2,1,0:T(8,128)(2,1)} custom-call(f32[16,16,128]{2,1,0:T(8,128)} %bitcast.14, bf16[4,256,512]{2,1,0:T(8,128)(2,1)} %constant.8.clone.refs_1_.refs_2_, bf16[64,32,16,128]{3,2,1,0:T(8,128)(2,1)} %bitcast.11), custom_call_target="tpu_custom_call" | custom-call | flops 274877906944 | bytes 17825792 | tf_op jit(solution)/shard_map/pallas_call | solution.py:135
  37.0 18.8 %collective-permute-done.refs_4_ = bf16[64,8,16,128]{3,2,1,0:T(8,128)(2,1)} collective-permute-done((bf16[64,8,16,128]{3,2,1,0:T(8,128)(2,1)}, bf16[64,8,16,128]{3,2,1,0:T(8,128)(2,1)}, u32[]{:S(2)}, u32[]{:S(2)}) %collective-permute-start) | collective-permute-done | bytes 2097184 | tf_op jit(solution)/shard_map/ppermute | solution.py:276
  55.8 10.8 %all-to-all-start = ((bf16[128,8,16,128]{3,2,1,0:T(8,128)(2,1)}), bf16[128,8,16,128]{3,2,1,0:T(8,128)(2,1)}, u32[]{:S(2)}, u32[]{:S(2)}) async-start(bf16[128,8,16,128]{3,2,1,0:T(8,128)(2,1)} %shard_map.37), calls=%async_computation | async-start | bytes 8388608 | tf_op jit(solution)/shard_map/all_to_all | solution.py:287
  66.5 0.0 collective-permute-done.1.refs_5_
  66.5 24.5 %shard_map.40 = bf16[128,8,16,128]{3,2,1,0:T(8,128)(2,1)} custom-call(f32[1]{0:T(128)} %bitcast.6.refs_0_, f32[16,16,128]{2,1,0:T(8,128)} %bitcast.15, bf16[4,256,512]{2,1,0:T(8,128)(2,1)} %constant.8.clone.refs_1_.refs_2_, bf16[64,32,16,128]{3,2,1,0:T(8,128)(2,1)} %bitcast.12, bf16[64,8,16,128]{3,2,1,0:T(8,128)(2,1)} %collective-permute-done.refs_4_, ...), custom_call_target="tpu_custom_call" | custom-call | flops 274877906944 | bytes 17825792 | tf_op jit(solution)/shard_map/pallas_call | solution.py:135
  91.1 27.4 %all-to-all-done.ref = bf16[128,8,16,128]{3,2,1,0:T(8,128)(2,1)} async-done(((bf16[128,8,16,128]{3,2,1,0:T(8,128)(2,1)}), bf16[128,8,16,128]{3,2,1,0:T(8,128)(2,1)}, u32[]{:S(2)}, u32[]{:S(2)}) %all-to-all-start) | async-done | bytes 4194336 | tf_op jit(solution)/shard_map/all_to_all | solution.py:287
  118.5 5.2 %all-to-all-start.1 = ((bf16[128,8,16,128]{3,2,1,0:T(8,128)(2,1)}), bf16[128,8,16,128]{3,2,1,0:T(8,128)(2,1)}, u32[]{:S(2)}, u32[]{:S(2)}) async-start(bf16[128,8,16,128]{3,2,1,0:T(8,128)(2,1)} %shard_map.40), calls=%async_computation.1 | async-start | bytes 8388608 | tf_op jit(solution)/shard_map/all_to_all | solution.py:288
  123.7 7.3 %shard_map.39.ready_ref = bf16[8,2,256,512]{3,2,1,0:T(8,128)(2,1)} custom-call(bf16[128,8,16,128]{3,2,1,0:T(8,128)(2,1)} %all-to-all-done.ref), custom_call_target="tpu_custom_call" | custom-call | flops 274877906944 | bytes 9437184 | tf_op jit(solution)/shard_map/pallas_call | solution.py:202
  131.0 44.6 %all-to-all-done.1.ref = bf16[128,8,16,128]{3,2,1,0:T(8,128)(2,1)} async-done(((bf16[128,8,16,128]{3,2,1,0:T(8,128)(2,1)}), bf16[128,8,16,128]{3,2,1,0:T(8,128)(2,1)}, u32[]{:S(2)}, u32[]{:S(2)}) %all-to-all-start.1) | async-done | bytes 4194336 | tf_op jit(solution)/shard_map/all_to_all | solution.py:288
  175.6 14.3 %shard_map.41 = f32[8,2,512,512]{3,2,1,0:T(8,128)} custom-call(bf16[8,2,256,512]{3,2,1,0:T(8,128)(2,1)} %shard_map.39.ready_ref, bf16[128,8,16,128]{3,2,1,0:T(8,128)(2,1)} %all-to-all-done.1.ref), custom_call_target="tpu_custom_call" | custom-call | flops 4294967296 | bytes 26214400 | tf_op jit(solution)/shard_map/pallas_call | solution.py:248
  (1 shorter events, 0.0 us)
Async XLA Ops:
  0.0 12.5 %copy-start = (f32[16,1024]{1,0:T(8,128)S(1)}, f32[16,1024]{1,0:T(8,128)}, u32[]{:S(2)}) copy-start(f32[16,1024]{1,0:T(8,128)} %param.4) | copy-start | bytes 196612
  3.7 62.9 %collective-permute-start.1 = (bf16[64,7,16,128]{3,2,1,0:T(8,128)(2,1)}, bf16[64,7,16,128]{3,2,1,0:T(8,128)(2,1)}, u32[]{:S(2)}, u32[]{:S(2)}) collective-permute-start(bf16[64,7,16,128]{3,2,1,0:T(8,128)(2,1)} %get-tuple-element.12), channel_id=1, source_target_pairs={{0,15},{1,0},{2,1},{3,2},{4,3},{5,4},{6,5},{7,6},{8,7},{9,8},{10,9... | collective-permute-start | bytes 5505032 | tf_op jit(solution)/shard_map/ppermute | solution.py:277
  9.9 45.9 %collective-permute-start = (bf16[64,8,16,128]{3,2,1,0:T(8,128)(2,1)}, bf16[64,8,16,128]{3,2,1,0:T(8,128)(2,1)}, u32[]{:S(2)}, u32[]{:S(2)}) collective-permute-start(bf16[64,8,16,128]{3,2,1,0:T(8,128)(2,1)} %get-tuple-element.9), channel_id=1, source_target_pairs={{0,1},{1,2},{2,3},{3,4},{4,5},{5,6},{6,7},{7,8},{8,9},{9,10},{10,1... | collective-permute-start | bytes 6291464 | tf_op jit(solution)/shard_map/ppermute | solution.py:276
  55.8 62.7 %all-to-all-start = ((bf16[128,8,16,128]{3,2,1,0:T(8,128)(2,1)}), bf16[128,8,16,128]{3,2,1,0:T(8,128)(2,1)}, u32[]{:S(2)}, u32[]{:S(2)}) async-start(bf16[128,8,16,128]{3,2,1,0:T(8,128)(2,1)} %shard_map.37), calls=%async_computation | async-start | bytes 8388608 | tf_op jit(solution)/shard_map/all_to_all | solution.py:287
  118.5 57.1 %all-to-all-start.1 = ((bf16[128,8,16,128]{3,2,1,0:T(8,128)(2,1)}), bf16[128,8,16,128]{3,2,1,0:T(8,128)(2,1)}, u32[]{:S(2)}, u32[]{:S(2)}) async-start(bf16[128,8,16,128]{3,2,1,0:T(8,128)(2,1)} %shard_map.40), calls=%async_computation.1 | async-start | bytes 8388608 | tf_op jit(solution)/shard_map/all_to_all | solution.py:288

commit v3 on v2

--- a/solution.py
+++ b/solution.py
@@ -12,6 +12,8 @@
 
 AXES = ("station", "tm")
 BEFORE = 8
+INNER = tuple(range(23, 31)), tuple(range(31, 39))
+OUTER = tuple(range(15, 23)), tuple(range(39, 47))
 INPUT_BLOCK = 16
 PITCH = 24
 EDGE_STEPS = 2
@@ -27,46 +29,51 @@
     return parts.astype(ml_dtypes.bfloat16)
 
 
-def filter_group(outputs, first, last, get, taps_ref, keep, wrap):
+def filter_terms(outputs, first, last, get, taps_ref, start):
     tap_count = taps_ref.shape[0]
-    own = [None] * len(outputs)
-    for e in range(first, last):
-        if wrap is not None and e == wrap:
-            own = [a if f < wrap else a * keep for f, a in zip(outputs, own)]
+    sums = list(start)
+    for e in range(max(first, outputs[0] - tap_count + 1), min(last, outputs[-1] + 1)):
         value = get(e).astype(jnp.float32)
         for n, f in enumerate(outputs):
             if 0 <= f - e < tap_count:
                 term = taps_ref[f - e] * value
-                own[n] = term if own[n] is None else own[n] + term
-    return own
-
-
-def channelize_body(groups, wrap, own_first, own_count, *refs):
-    if wrap is None:
-        taps_ref, table_ref, own_ref, out_ref, filtered, data, turned = refs
-        keep = None
-        before_ref = after_ref = None
-    else:
-        (keep_ref, taps_ref, table_ref, own_ref, before_ref, after_ref, out_ref, filtered, data, turned) = refs
-        keep = keep_ref[0]
+                sums[n] = term if sums[n] is None else sums[n] + term
+    return sums
+
+
+def filter_own(i, wrap, keep, taps_ref, own_ref, partial_ref, filtered):
+    def get(e):
+        return own_ref[i, e - BEFORE]
+
+    for g, outputs in enumerate(INNER):
+        for n, value in enumerate(filter_terms(outputs, BEFORE, wrap, get, taps_ref, [None] * 8)):
+            filtered[8 * g + n, pl.ds(pl.multiple_of(i * PITCH, 8), 16), :] = value
+    for g, outputs in enumerate(OUTER):
+        for n, value in enumerate(filter_terms(outputs, BEFORE, wrap, get, taps_ref, [None] * 8)):
+            partial_ref[i, 8 * g + n] = value if outputs[n] < wrap else value * keep
+
+
+def filter_halo(i, wrap, taps_ref, partial_ref, before_ref, after_ref, filtered):
+    parts = (0, BEFORE, lambda e: before_ref[i, e]), (wrap, wrap + after_ref.shape[1], lambda e: after_ref[i, e - wrap])
+    for g, (outputs, (first, last, get)) in enumerate(zip(OUTER, parts)):
+        start = [partial_ref[i, 8 * g + n] for n in range(8)]
+        for n, value in enumerate(filter_terms(outputs, first, last, get, taps_ref, start)):
+            filtered[8 * g + n, pl.ds(pl.multiple_of(i * PITCH, 8), 16), :] = value
+
+
+def channelize_body(wrap, halo, *refs):
     step = pl.program_id(0)
     rows = INPUT_BLOCK
+    if halo:
+        taps_ref, table_ref, partial_ref, before_ref, after_ref, out_ref, filtered, data, turned = refs
+    else:
+        keep_ref, taps_ref, table_ref, own_ref, out_ref, partial_ref, filtered, data, turned = refs
 
     def filter_input(i, _):
-        def get(e):
-            if e < own_first:
-                return before_ref[i, e]
-            if e < own_first + own_count:
-                return own_ref[i, e - own_first]
-            return after_ref[i, e - own_first - own_count]
-
-        done = 0
-        for outputs in groups:
-            first = outputs[0] - (taps_ref.shape[0] - 1)
-            values = filter_group(outputs, first, outputs[-1] + 1, get, taps_ref, keep, wrap)
-            for n, value in enumerate(values):
-                filtered[done + n, pl.ds(pl.multiple_of(i * PITCH, 8), 16), :] = value
-            done += len(outputs)
+        if halo:
+            filter_halo(i, wrap, taps_ref, partial_ref, before_ref, after_ref, filtered)
+        else:
+            filter_own(i, wrap, keep_ref[0], taps_ref, own_ref, partial_ref, filtered)
         return 0
 
     lax.fori_loop(0, rows, filter_input, 0)
@@ -121,23 +128,29 @@
         lax.fori_loop(0, 64, write, 0)
 
 
-def channelize(groups, wrap, own_first, keep, taps, table, own, before, after, devices):
-    inputs, own_count = own.shape[0], own.shape[1]
+def channelize(taps, table, devices, wrap, own=None, keep=None, partial=None, halo=()):
+    inputs = (partial if own is None else own).shape[0]
     whole = pl.BlockSpec(memory_space=pltpu.VMEM)
 
-    def per_input(array):
-        return pl.BlockSpec((INPUT_BLOCK,) + array.shape[1:], lambda s: (s, 0, 0, 0))
-
-    operands, specs = [taps, table, own], [whole, whole, per_input(own)]
-    if wrap is not None:
-        operands = [keep] + operands + [before, after]
-        specs = [pl.BlockSpec(memory_space=pltpu.SMEM)] + specs + [per_input(before), per_input(after)]
+    def per_input(shape):
+        return pl.BlockSpec((INPUT_BLOCK,) + shape[1:], lambda s: (s, 0, 0, 0))
+
+    sums = jax.ShapeDtypeStruct((inputs, 16, 16, 128), jnp.float32)
+    blocks = jax.ShapeDtypeStruct((devices, 8, 16, 128), jnp.bfloat16)
+    if own is None:
+        operands = [taps, table, partial, *halo]
+        specs = [whole, whole] + [per_input(a.shape) for a in operands[2:]]
+        out_shape, out_specs = blocks, whole
+    else:
+        operands = [keep, taps, table, own]
+        specs = [pl.BlockSpec(memory_space=pltpu.SMEM), whole, whole, per_input(own.shape)]
+        out_shape, out_specs = [blocks, sums], [whole, per_input(sums.shape)]
     return pl.pallas_call(
-        functools.partial(channelize_body, groups, wrap, own_first, own_count),
+        functools.partial(channelize_body, wrap, own is None),
         grid=(inputs // INPUT_BLOCK,),
         in_specs=specs,
-        out_specs=whole,
-        out_shape=jax.ShapeDtypeStruct((devices, 8, 16, 128), jnp.bfloat16),
+        out_specs=out_specs,
+        out_shape=out_shape,
         scratch_shapes=[
             pltpu.VMEM((16, INPUT_BLOCK * PITCH, 128), jnp.float32),
             pltpu.VMEM((4, 16, 2, 64, 512), jnp.bfloat16),
@@ -279,11 +292,9 @@
     table = jnp.asarray(transform_rows(nfft))
     keep = (lax.axis_index("tm") < n_tm - 1).astype(jnp.float32).reshape(1)
 
-    inner = [tuple(range(15, 23)), tuple(range(23, 31))]
-    outer = [tuple(range(15, 23)), tuple(range(39, 47))]
-    first = channelize(inner, None, 0, None, taps_rows, table, own, None, None, devices)
-    first, before = lax.optimization_barrier((first, before))
-    second = channelize(outer, BEFORE + frames, BEFORE, keep, taps_rows, table, own, before, after, devices)
+    wrap = BEFORE + frames
+    first, partial = channelize(taps_rows, table, devices, wrap, own=own, keep=keep)
+    second = channelize(taps_rows, table, devices, wrap, partial=partial, halo=(before, after))
     first = lax.all_to_all(first, AXES, 0, 0, tiled=True)
     second = lax.all_to_all(second, AXES, 0, 0, tiled=True)
     return correlate(unpack(first), second, n_tm * frames)

time: 191 us -> 185 us (0.969)
  waiting for transfers between devices: 90.8 us -> 79.5 us
  starting transfers between devices: 24.8 us -> 29.1 us
    ppermute x1, waiting for transfers between devices: 18.8 us -> 9.09 us  [per_device(): before = lax.ppermute(tail, 'tm', up)]
    all_to_all x1, starting transfers between devices: 5.17 us -> 12.1 us  [per_device(): second = lax.all_to_all(second, AXES, 0, 0, tiled=True)]
    all_to_all x1, starting transfers between devices: 10.8 us -> 8.15 us  [per_device(): first = lax.all_to_all(first, AXES, 0, 0, tiled=True)]
  transfers between devices with their start and end apart: 4 -> 4, of which waited for: 3 -> 3; matrix products, arithmetic and copies ran while one was open for 0% -> 0% of each run, Pallas kernels for 29% -> 31%
where the time goes in v3:
time: 185 us; the launch traced here: 184 us
  waiting for transfers between devices  79.5 us (43%)
  Pallas kernels  74.5 us (40%)
  starting transfers between devices  29.1 us (16%)
    pallas_call x2, Pallas kernels, channelize(): pl.pallas_call(functools.partial(channelize_body, wrap, own is None), gri...  49.3 us
    all_to_all x1, waiting for transfers between devices, per_device(): second = lax.all_to_all(second, AXES, 0, 0, tiled=True)  44.6 us
    all_to_all x1, waiting for transfers between devices, per_device(): first = lax.all_to_all(first, AXES, 0, 0, tiled=True)  25.8 us
    pallas_call x1, Pallas kernels, correlate(): pl.pallas_call(functools.partial(correlate_body, 1.0 / frames), grid=(cha...  14.3 us
    all_to_all x1, starting transfers between devices, per_device(): second = lax.all_to_all(second, AXES, 0, 0, tiled=True)  12.1 us
    ppermute x1, waiting for transfers between devices, per_device(): before = lax.ppermute(tail, 'tm', up)  9.09 us
    all_to_all x1, starting transfers between devices, per_device(): first = lax.all_to_all(first, AXES, 0, 0, tiled=True)  8.15 us
    pallas_call x1, Pallas kernels, unpack(): pl.pallas_call(unpack_body, grid=(channels,), in_specs=[received(spectra)...  7.34 us
  transfers between devices with their start and end apart: 4, of which 3 were waited for; matrix products, arithmetic and copies ran while one was open for 0% of the time, Pallas kernels for 31%

profile of v3, /device:TPU:7, one launch (start us, length us, event | category | flops | bytes accessed | tf_op | source)
XLA Modules:
  0.0 183.8 jit_solution(9744001492480729249)
XLA Ops:
  0.0 0.0 copy-start
  0.0 3.6 %shard_map.39 = (bf16[64,7,16,128]{3,2,1,0:T(8,128)(2,1)}, bf16[64,8,16,128]{3,2,1,0:T(8,128)(2,1)}) custom-call(bf16[64,32,16,128]{3,2,1,0:T(8,128)(2,1)} %bitcast.9, bf16[64,32,16,128]{3,2,1,0:T(8,128)(2,1)} %bitcast.10), custom_call_target="tpu_custom_call" | custom-call | tf_op jit(solution)/shard_map/pallas_call | solution.py:176
  3.6 6.2 %collective-permute-start.1 = (bf16[64,7,16,128]{3,2,1,0:T(8,128)(2,1)}, bf16[64,7,16,128]{3,2,1,0:T(8,128)(2,1)}, u32[]{:S(2)}, u32[]{:S(2)}) collective-permute-start(bf16[64,7,16,128]{3,2,1,0:T(8,128)(2,1)} %get-tuple-element.12), channel_id=1, source_target_pairs={{0,15},{1,0},{2,1},{3,2},{4,3},{5,4},{6,5},{7,6},{8,7},{9,8},{10,9... | collective-permute-start | bytes 5505032 | tf_op jit(solution)/shard_map/ppermute | solution.py:290
  9.8 2.6 %collective-permute-start = (bf16[64,8,16,128]{3,2,1,0:T(8,128)(2,1)}, bf16[64,8,16,128]{3,2,1,0:T(8,128)(2,1)}, u32[]{:S(2)}, u32[]{:S(2)}) collective-permute-start(bf16[64,8,16,128]{3,2,1,0:T(8,128)(2,1)} %get-tuple-element.11), channel_id=1, source_target_pairs={{0,1},{1,2},{2,3},{3,4},{4,5},{5,6},{6,7},{7,8},{8,9},{9,10},{10,1... | collective-permute-start | bytes 6291464 | tf_op jit(solution)/shard_map/ppermute | solution.py:289
  12.4 0.0 copy-done
  12.5 0.7 broadcast_in_dim.3
  13.2 31.5 %shard_map.37 = (bf16[128,8,16,128]{3,2,1,0:T(8,128)(2,1)}, f32[64,16,16,128]{3,2,1,0:T(8,128)}) custom-call(f32[1]{0:T(128)} %bitcast.refs_0_, f32[16,16,128]{2,1,0:T(8,128)} %bitcast.13, bf16[4,256,512]{2,1,0:T(8,128)(2,1)} %constant.8.clone.refs_2_.refs_1_, bf16[64,32,16,128]{3,2,1,0:T(8,128)(2,1)} %bitcast.11), custom_call_target="tpu_custom_call" | custom-call | flops 274877906944 | bytes 17825792 | tf_op jit(solution)/shard_map/pallas_call | solution.py:148
  44.6 8.1 %all-to-all-start = ((bf16[128,8,16,128]{3,2,1,0:T(8,128)(2,1)}), bf16[128,8,16,128]{3,2,1,0:T(8,128)(2,1)}, u32[]{:S(2)}, u32[]{:S(2)}) async-start(bf16[128,8,16,128]{3,2,1,0:T(8,128)(2,1)} %get-tuple-element.9), calls=%async_computation | async-start | bytes 8388608 | tf_op jit(solution)/shard_map/all_to_all | solution.py:298
  52.8 0.0 collective-permute-done.1.refs_4_
  52.8 9.1 %collective-permute-done.refs_3_ = bf16[64,8,16,128]{3,2,1,0:T(8,128)(2,1)} collective-permute-done((bf16[64,8,16,128]{3,2,1,0:T(8,128)(2,1)}, bf16[64,8,16,128]{3,2,1,0:T(8,128)(2,1)}, u32[]{:S(2)}, u32[]{:S(2)}) %collective-permute-start) | collective-permute-done | bytes 2097184 | tf_op jit(solution)/shard_map/ppermute | solution.py:289
  61.9 17.8 %shard_map.40 = bf16[128,8,16,128]{3,2,1,0:T(8,128)(2,1)} custom-call(f32[16,16,128]{2,1,0:T(8,128)} %bitcast.14, bf16[4,256,512]{2,1,0:T(8,128)(2,1)} %constant.8.clone.refs_2_.refs_1_, f32[64,16,16,128]{3,2,1,0:T(8,128)} %get-tuple-element.10.refs_2_, bf16[64,8,16,128]{3,2,1,0:T(8,128)(2,1)} %collective-permute-done.refs_3_, ...), custom_call_target="tpu_custom_call" | custom-call | flops 274877906944 | bytes 17825792 | tf_op jit(solution)/shard_map/pallas_call | solution.py:148
  79.7 25.8 %all-to-all-done.ref = bf16[128,8,16,128]{3,2,1,0:T(8,128)(2,1)} async-done(((bf16[128,8,16,128]{3,2,1,0:T(8,128)(2,1)}), bf16[128,8,16,128]{3,2,1,0:T(8,128)(2,1)}, u32[]{:S(2)}, u32[]{:S(2)}) %all-to-all-start) | async-done | bytes 4194336 | tf_op jit(solution)/shard_map/all_to_all | solution.py:298
  105.5 12.1 %all-to-all-start.1 = ((bf16[128,8,16,128]{3,2,1,0:T(8,128)(2,1)}), bf16[128,8,16,128]{3,2,1,0:T(8,128)(2,1)}, u32[]{:S(2)}, u32[]{:S(2)}) async-start(bf16[128,8,16,128]{3,2,1,0:T(8,128)(2,1)} %shard_map.40), calls=%async_computation.1 | async-start | bytes 8388608 | tf_op jit(solution)/shard_map/all_to_all | solution.py:299
  117.6 7.3 %shard_map.38.ready_ref = bf16[8,2,256,512]{3,2,1,0:T(8,128)(2,1)} custom-call(bf16[128,8,16,128]{3,2,1,0:T(8,128)(2,1)} %all-to-all-done.ref), custom_call_target="tpu_custom_call" | custom-call | flops 274877906944 | bytes 9437184 | tf_op jit(solution)/shard_map/pallas_call | solution.py:215
  124.9 44.6 %all-to-all-done.1.ref = bf16[128,8,16,128]{3,2,1,0:T(8,128)(2,1)} async-done(((bf16[128,8,16,128]{3,2,1,0:T(8,128)(2,1)}), bf16[128,8,16,128]{3,2,1,0:T(8,128)(2,1)}, u32[]{:S(2)}, u32[]{:S(2)}) %all-to-all-start.1) | async-done | bytes 4194336 | tf_op jit(solution)/shard_map/all_to_all | solution.py:299
  169.5 14.3 %shard_map.41 = f32[8,2,512,512]{3,2,1,0:T(8,128)} custom-call(bf16[8,2,256,512]{3,2,1,0:T(8,128)(2,1)} %shard_map.38.ready_ref, bf16[128,8,16,128]{3,2,1,0:T(8,128)(2,1)} %all-to-all-done.1.ref), custom_call_target="tpu_custom_call" | custom-call | flops 4294967296 | bytes 26214400 | tf_op jit(solution)/shard_map/pallas_call | solution.py:261
  (1 shorter events, 0.0 us)
Async XLA Ops:
  0.0 12.4 %copy-start = (f32[16,1024]{1,0:T(8,128)S(1)}, f32[16,1024]{1,0:T(8,128)}, u32[]{:S(2)}) copy-start(f32[16,1024]{1,0:T(8,128)} %param.4) | copy-start | bytes 196612
  3.6 49.2 %collective-permute-start.1 = (bf16[64,7,16,128]{3,2,1,0:T(8,128)(2,1)}, bf16[64,7,16,128]{3,2,1,0:T(8,128)(2,1)}, u32[]{:S(2)}, u32[]{:S(2)}) collective-permute-start(bf16[64,7,16,128]{3,2,1,0:T(8,128)(2,1)} %get-tuple-element.12), channel_id=1, source_target_pairs={{0,15},{1,0},{2,1},{3,2},{4,3},{5,4},{6,5},{7,6},{8,7},{9,8},{10,9... | collective-permute-start | bytes 5505032 | tf_op jit(solution)/shard_map/ppermute | solution.py:290
  9.8 52.1 %collective-permute-start = (bf16[64,8,16,128]{3,2,1,0:T(8,128)(2,1)}, bf16[64,8,16,128]{3,2,1,0:T(8,128)(2,1)}, u32[]{:S(2)}, u32[]{:S(2)}) collective-permute-start(bf16[64,8,16,128]{3,2,1,0:T(8,128)(2,1)} %get-tuple-element.11), channel_id=1, source_target_pairs={{0,1},{1,2},{2,3},{3,4},{4,5},{5,6},{6,7},{7,8},{8,9},{9,10},{10,1... | collective-permute-start | bytes 6291464 | tf_op jit(solution)/shard_map/ppermute | solution.py:289
  44.6 60.9 %all-to-all-start = ((bf16[128,8,16,128]{3,2,1,0:T(8,128)(2,1)}), bf16[128,8,16,128]{3,2,1,0:T(8,128)(2,1)}, u32[]{:S(2)}, u32[]{:S(2)}) async-start(bf16[128,8,16,128]{3,2,1,0:T(8,128)(2,1)} %get-tuple-element.9), calls=%async_computation | async-start | bytes 8388608 | tf_op jit(solution)/shard_map/all_to_all | solution.py:298
  105.5 64.0 %all-to-all-start.1 = ((bf16[128,8,16,128]{3,2,1,0:T(8,128)(2,1)}), bf16[128,8,16,128]{3,2,1,0:T(8,128)(2,1)}, u32[]{:S(2)}, u32[]{:S(2)}) async-start(bf16[128,8,16,128]{3,2,1,0:T(8,128)(2,1)} %shard_map.40), calls=%async_computation.1 | async-start | bytes 8388608 | tf_op jit(solution)/shard_map/all_to_all | solution.py:299

commit v4 on v3

--- a/solution.py
+++ b/solution.py
@@ -15,7 +15,7 @@
 INNER = tuple(range(23, 31)), tuple(range(31, 39))
 OUTER = tuple(range(15, 23)), tuple(range(39, 47))
 INPUT_BLOCK = 16
-PITCH = 24
+PITCH = TURN = 24
 EDGE_STEPS = 2
 VMEM_BYTES = 60 * 1024 * 1024
 
@@ -114,18 +114,20 @@
                 result = lax.dot_general(
                     table_ref[p], pair, (((1,), (1,)), ((), ())), preferred_element_type=jnp.float32
                 )
-                turned[pl.ds(16 * p + 2 * n, 256, stride=64), :] = result[:, :128]
-                turned[pl.ds(16 * p + 2 * n + 1, 256, stride=64), :] = result[:, 128:]
+                turned[pl.ds(256 * TURN * p + 2 * n, 256, stride=TURN), :] = result[:, :128]
+                turned[pl.ds(256 * TURN * p + 2 * n + 1, 256, stride=TURN), :] = result[:, 128:]
             return 0
 
         lax.fori_loop(0, 8, transform, 0)
 
         def write(d, _):
-            block = turned[pl.ds(pl.multiple_of(d * 256, 256), 256), :]
-            out_ref[pl.ds(2 * d, 2)] = block.reshape(2, 8, 16, 128).astype(jnp.bfloat16)
+            for q in range(2):
+                for p in range(4):
+                    row = pl.multiple_of(2 * TURN * d, 8) + TURN * (256 * p + q)
+                    out_ref[d, 4 * q + p] = turned[pl.ds(row, 16), :].astype(jnp.bfloat16)
             return 0
 
-        lax.fori_loop(0, 64, write, 0)
+        lax.fori_loop(0, 128, write, 0, unroll=4)
 
 
 def channelize(taps, table, devices, wrap, own=None, keep=None, partial=None, halo=()):
@@ -154,7 +156,7 @@
         scratch_shapes=[
             pltpu.VMEM((16, INPUT_BLOCK * PITCH, 128), jnp.float32),
             pltpu.VMEM((4, 16, 2, 64, 512), jnp.bfloat16),
-            pltpu.VMEM((1024 * 16, 128), jnp.float32),
+            pltpu.VMEM((1024 * TURN, 128), jnp.float32),
         ],
         compiler_params=pltpu.CompilerParams(vmem_limit_bytes=VMEM_BYTES),
         cost_estimate=pl.CostEstimate(
@@ -163,27 +165,21 @@
     )(*operands)
 
 
-def edges_body(first_ref, last_ref, head_ref, tail_ref):
-    head_ref[...] = first_ref[:, : head_ref.shape[1]]
-    tail_ref[...] = last_ref[...]
-
-
-def edges(own, head):
-    inputs, frames = own.shape[:2]
+def edge_body(first, source_ref, out_ref):
+    out_ref[...] = source_ref[:, first : first + out_ref.shape[1]]
+
+
+def edge(own, block, first, count):
+    inputs = own.shape[0]
     rows = inputs // EDGE_STEPS
-    shapes = [(inputs, count) + own.shape[2:] for count in (head, BEFORE)]
-    last = frames // BEFORE - 1
     return pl.pallas_call(
-        edges_body,
+        functools.partial(edge_body, first),
         grid=(EDGE_STEPS,),
-        in_specs=[
-            pl.BlockSpec((rows, BEFORE) + own.shape[2:], lambda s: (s, 0, 0, 0)),
-            pl.BlockSpec((rows, BEFORE) + own.shape[2:], lambda s: (s, last, 0, 0)),
-        ],
-        out_specs=[pl.BlockSpec((rows,) + shape[1:], lambda s: (s, 0, 0, 0)) for shape in shapes],
-        out_shape=[jax.ShapeDtypeStruct(shape, own.dtype) for shape in shapes],
+        in_specs=[pl.BlockSpec((rows, BEFORE) + own.shape[2:], lambda s: (s, block, 0, 0))],
+        out_specs=pl.BlockSpec((rows, count) + own.shape[2:], lambda s: (s, 0, 0, 0)),
+        out_shape=jax.ShapeDtypeStruct((inputs, count) + own.shape[2:], own.dtype),
         compiler_params=pltpu.CompilerParams(vmem_limit_bytes=VMEM_BYTES),
-    )(own, own)
+    )(own)
 
 
 def unpack_pair(low, high):
@@ -285,8 +281,9 @@
     own = blocked(voltages)
     up = [(d, d + 1) for d in range(n_tm - 1)]
     down = [(d, (d - 1) % n_tm) for d in range(n_tm)]
-    head, tail = edges(own, after_count)
+    tail = edge(own, frames // BEFORE - 1, 0, BEFORE)
     before = lax.ppermute(tail, "tm", up)
+    head = edge(lax.optimization_barrier((own, tail))[0], 0, 0, after_count)
     after = lax.ppermute(head, "tm", down)
     taps_rows = jnp.repeat(taps.reshape(tap_count, 8, 1, 128), 2, axis=2).reshape(tap_count, 16, 128)
     table = jnp.asarray(transform_rows(nfft))

time: 185 us -> 177 us (0.957)
  starting transfers between devices: 29.1 us -> 21.4 us
  waiting for transfers between devices: 79.5 us -> 84.5 us
  Pallas kernels: 74.5 us -> 70 us
    ppermute x1, waiting for transfers between devices: 0.01 us -> 9.42 us  [per_device(): after = lax.ppermute(head, 'tm', down)]
    ppermute x1, waiting for transfers between devices: 9.09 us -> 0.01 us  [per_device(): before = lax.ppermute(tail, 'tm', up)]
    pallas_call x2, Pallas kernels: 49.3 us -> 43.2 us  [channelize(): pl.pallas_call(functools.partial(channelize_body, wrap, own is None), gri...]
    all_to_all x1, starting transfers between devices: 12.1 us -> 6.04 us  [per_device(): second = lax.all_to_all(second, AXES, 0, 0, tiled=True)]
    all_to_all x1, waiting for transfers between devices: 25.8 us -> 30.5 us  [per_device(): first = lax.all_to_all(first, AXES, 0, 0, tiled=True)]
    ppermute x1, starting transfers between devices: 6.21 us -> 2.99 us  [per_device(): after = lax.ppermute(head, 'tm', down)]
    ppermute x1, starting transfers between devices: 2.61 us -> 4.65 us  [per_device(): before = lax.ppermute(tail, 'tm', up)]
    pallas_call x1 -> x2, Pallas kernels: 3.61 us -> 5.17 us  [edge(): pl.pallas_call(functools.partial(edge_body, first), grid=(EDGE_STEPS,), i...]
  transfers between devices with their start and end apart: 4 -> 4, of which waited for: 3 -> 3; matrix products, arithmetic and copies ran while one was open for 0% -> 0% of each run, Pallas kernels for 31% -> 30%
where the time goes in v4:
time: 177 us
  waiting for transfers between devices  84.5 us (48%)
  Pallas kernels  70 us (40%)
  starting transfers between devices  21.4 us (12%)
    all_to_all x1, waiting for transfers between devices, per_device(): second = lax.all_to_all(second, AXES, 0, 0, tiled=True)  44.6 us
    pallas_call x2, Pallas kernels, channelize(): pl.pallas_call(functools.partial(channelize_body, wrap, own is None), gri...  43.2 us
    all_to_all x1, waiting for transfers between devices, per_device(): first = lax.all_to_all(first, AXES, 0, 0, tiled=True)  30.5 us
    pallas_call x1, Pallas kernels, correlate(): pl.pallas_call(functools.partial(correlate_body, 1.0 / frames), grid=(cha...  14.3 us
    ppermute x1, waiting for transfers between devices, per_device(): after = lax.ppermute(head, 'tm', down)  9.42 us
    all_to_all x1, starting transfers between devices, per_device(): first = lax.all_to_all(first, AXES, 0, 0, tiled=True)  7.69 us
    pallas_call x1, Pallas kernels, unpack(): pl.pallas_call(unpack_body, grid=(channels,), in_specs=[received(spectra)...  7.33 us
    all_to_all x1, starting transfers between devices, per_device(): second = lax.all_to_all(second, AXES, 0, 0, tiled=True)  6.04 us
  transfers between devices with their start and end apart: 4, of which 3 were waited for; matrix products, arithmetic and copies ran while one was open for 0% of the time, Pallas kernels for 30%

profile of v4, /device:TPU:7, one launch (start us, length us, event | category | flops | bytes accessed | tf_op | source)
XLA Modules:
  0.0 176.6 jit_solution(15644487846834458878)
XLA Ops:
  0.0 2.7 %shard_map.39 = bf16[64,8,16,128]{3,2,1,0:T(8,128)(2,1)} custom-call(bf16[64,32,16,128]{3,2,1,0:T(8,128)(2,1)} %bitcast.9), custom_call_target="tpu_custom_call" | custom-call | tf_op jit(solution)/shard_map/pallas_call | solution.py:175
  2.7 0.0 copy-start
  2.7 4.7 %collective-permute-start = (bf16[64,8,16,128]{3,2,1,0:T(8,128)(2,1)}, bf16[64,8,16,128]{3,2,1,0:T(8,128)(2,1)}, u32[]{:S(2)}, u32[]{:S(2)}) collective-permute-start(bf16[64,8,16,128]{3,2,1,0:T(8,128)(2,1)} %shard_map.39), channel_id=1, source_target_pairs={{0,1},{1,2},{2,3},{3,4},{4,5},{5,6},{6,7},{7,8},{8,9},{9,10},{10,1... | collective-permute-start | bytes 6291464 | tf_op jit(solution)/shard_map/ppermute | solution.py:285
  7.3 2.5 %shard_map.40 = bf16[64,7,16,128]{3,2,1,0:T(8,128)(2,1)} custom-call(bf16[64,32,16,128]{3,2,1,0:T(8,128)(2,1)} %bitcast.10), custom_call_target="tpu_custom_call" | custom-call | tf_op jit(solution)/shard_map/pallas_call | solution.py:175
  9.8 3.0 %collective-permute-start.1 = (bf16[64,7,16,128]{3,2,1,0:T(8,128)(2,1)}, bf16[64,7,16,128]{3,2,1,0:T(8,128)(2,1)}, u32[]{:S(2)}, u32[]{:S(2)}) collective-permute-start(bf16[64,7,16,128]{3,2,1,0:T(8,128)(2,1)} %shard_map.40), channel_id=1, source_target_pairs={{0,15},{1,0},{2,1},{3,2},{4,3},{5,4},{6,5},{7,6},{8,7},{9,8},{10,9... | collective-permute-start | bytes 5505032 | tf_op jit(solution)/shard_map/ppermute | solution.py:287
  12.8 0.0 copy-done
  12.8 0.7 broadcast_in_dim.3
  13.5 28.4 %shard_map.37 = (bf16[128,8,16,128]{3,2,1,0:T(8,128)(2,1)}, f32[64,16,16,128]{3,2,1,0:T(8,128)}) custom-call(f32[1]{0:T(128)} %bitcast.refs_0_, f32[16,16,128]{2,1,0:T(8,128)} %bitcast.13, bf16[4,256,512]{2,1,0:T(8,128)(2,1)} %constant.8.clone.refs_2_.refs_1_, bf16[64,32,16,128]{3,2,1,0:T(8,128)(2,1)} %bitcast.11), custom_call_target="tpu_custom_call" | custom-call | flops 274877906944 | bytes 17825792 | tf_op jit(solution)/shard_map/pallas_call | solution.py:150
  41.9 7.7 %all-to-all-start = ((bf16[128,8,16,128]{3,2,1,0:T(8,128)(2,1)}), bf16[128,8,16,128]{3,2,1,0:T(8,128)(2,1)}, u32[]{:S(2)}, u32[]{:S(2)}) async-start(bf16[128,8,16,128]{3,2,1,0:T(8,128)(2,1)} %get-tuple-element.8), calls=%async_computation | async-start | bytes 8388608 | tf_op jit(solution)/shard_map/all_to_all | solution.py:295
  49.6 9.4 %collective-permute-done.1.refs_4_ = bf16[64,7,16,128]{3,2,1,0:T(8,128)(2,1)} collective-permute-done((bf16[64,7,16,128]{3,2,1,0:T(8,128)(2,1)}, bf16[64,7,16,128]{3,2,1,0:T(8,128)(2,1)}, u32[]{:S(2)}, u32[]{:S(2)}) %collective-permute-start.1) | collective-permute-done | bytes 1835040 | tf_op jit(solution)/shard_map/ppermute | solution.py:287
  59.1 0.0 collective-permute-done.refs_3_
  59.1 14.8 %shard_map.41 = bf16[128,8,16,128]{3,2,1,0:T(8,128)(2,1)} custom-call(f32[16,16,128]{2,1,0:T(8,128)} %bitcast.14, bf16[4,256,512]{2,1,0:T(8,128)(2,1)} %constant.8.clone.refs_2_.refs_1_, f32[64,16,16,128]{3,2,1,0:T(8,128)} %get-tuple-element.9.refs_2_, bf16[64,8,16,128]{3,2,1,0:T(8,128)(2,1)} %collective-permute-done.refs_3_, ...), custom_call_target="tpu_custom_call" | custom-call | flops 274877906944 | bytes 17825792 | tf_op jit(solution)/shard_map/pallas_call | solution.py:150
  73.8 30.5 %all-to-all-done.ref = bf16[128,8,16,128]{3,2,1,0:T(8,128)(2,1)} async-done(((bf16[128,8,16,128]{3,2,1,0:T(8,128)(2,1)}), bf16[128,8,16,128]{3,2,1,0:T(8,128)(2,1)}, u32[]{:S(2)}, u32[]{:S(2)}) %all-to-all-start) | async-done | bytes 4194336 | tf_op jit(solution)/shard_map/all_to_all | solution.py:295
  104.3 6.0 %all-to-all-start.1 = ((bf16[128,8,16,128]{3,2,1,0:T(8,128)(2,1)}), bf16[128,8,16,128]{3,2,1,0:T(8,128)(2,1)}, u32[]{:S(2)}, u32[]{:S(2)}) async-start(bf16[128,8,16,128]{3,2,1,0:T(8,128)(2,1)} %shard_map.41), calls=%async_computation.1 | async-start | bytes 8388608 | tf_op jit(solution)/shard_map/all_to_all | solution.py:296
  110.4 7.3 %shard_map.38.ready_ref = bf16[8,2,256,512]{3,2,1,0:T(8,128)(2,1)} custom-call(bf16[128,8,16,128]{3,2,1,0:T(8,128)(2,1)} %all-to-all-done.ref), custom_call_target="tpu_custom_call" | custom-call | flops 274877906944 | bytes 9437184 | tf_op jit(solution)/shard_map/pallas_call | solution.py:211
  117.7 44.6 %all-to-all-done.1.ref = bf16[128,8,16,128]{3,2,1,0:T(8,128)(2,1)} async-done(((bf16[128,8,16,128]{3,2,1,0:T(8,128)(2,1)}), bf16[128,8,16,128]{3,2,1,0:T(8,128)(2,1)}, u32[]{:S(2)}, u32[]{:S(2)}) %all-to-all-start.1) | async-done | bytes 4194336 | tf_op jit(solution)/shard_map/all_to_all | solution.py:296
  162.3 14.3 %shard_map.42 = f32[8,2,512,512]{3,2,1,0:T(8,128)} custom-call(bf16[8,2,256,512]{3,2,1,0:T(8,128)(2,1)} %shard_map.38.ready_ref, bf16[128,8,16,128]{3,2,1,0:T(8,128)(2,1)} %all-to-all-done.1.ref), custom_call_target="tpu_custom_call" | custom-call | flops 4294967296 | bytes 26214400 | tf_op jit(solution)/shard_map/pallas_call | solution.py:257
  (1 shorter events, 0.0 us)
Async XLA Ops:
  2.7 10.2 %copy-start = (f32[16,1024]{1,0:T(8,128)S(1)}, f32[16,1024]{1,0:T(8,128)}, u32[]{:S(2)}) copy-start(f32[16,1024]{1,0:T(8,128)} %param.4) | copy-start | bytes 196612
  2.7 56.4 %collective-permute-start = (bf16[64,8,16,128]{3,2,1,0:T(8,128)(2,1)}, bf16[64,8,16,128]{3,2,1,0:T(8,128)(2,1)}, u32[]{:S(2)}, u32[]{:S(2)}) collective-permute-start(bf16[64,8,16,128]{3,2,1,0:T(8,128)(2,1)} %shard_map.39), channel_id=1, source_target_pairs={{0,1},{1,2},{2,3},{3,4},{4,5},{5,6},{6,7},{7,8},{8,9},{9,10},{10,1... | collective-permute-start | bytes 6291464 | tf_op jit(solution)/shard_map/ppermute | solution.py:285
  9.8 49.2 %collective-permute-start.1 = (bf16[64,7,16,128]{3,2,1,0:T(8,128)(2,1)}, bf16[64,7,16,128]{3,2,1,0:T(8,128)(2,1)}, u32[]{:S(2)}, u32[]{:S(2)}) collective-permute-start(bf16[64,7,16,128]{3,2,1,0:T(8,128)(2,1)} %shard_map.40), channel_id=1, source_target_pairs={{0,15},{1,0},{2,1},{3,2},{4,3},{5,4},{6,5},{7,6},{8,7},{9,8},{10,9... | collective-permute-start | bytes 5505032 | tf_op jit(solution)/shard_map/ppermute | solution.py:287
  41.9 62.4 %all-to-all-start = ((bf16[128,8,16,128]{3,2,1,0:T(8,128)(2,1)}), bf16[128,8,16,128]{3,2,1,0:T(8,128)(2,1)}, u32[]{:S(2)}, u32[]{:S(2)}) async-start(bf16[128,8,16,128]{3,2,1,0:T(8,128)(2,1)} %get-tuple-element.8), calls=%async_computation | async-start | bytes 8388608 | tf_op jit(solution)/shard_map/all_to_all | solution.py:295
  104.3 58.0 %all-to-all-start.1 = ((bf16[128,8,16,128]{3,2,1,0:T(8,128)(2,1)}), bf16[128,8,16,128]{3,2,1,0:T(8,128)(2,1)}, u32[]{:S(2)}, u32[]{:S(2)}) async-start(bf16[128,8,16,128]{3,2,1,0:T(8,128)(2,1)} %shard_map.41), calls=%async_computation.1 | async-start | bytes 8388608 | tf_op jit(solution)/shard_map/all_to_all | solution.py:296

commit v5 on v4

--- a/solution.py
+++ b/solution.py
@@ -17,6 +17,7 @@
 INPUT_BLOCK = 16
 PITCH = TURN = 24
 EDGE_STEPS = 2
+CHANNEL_BLOCK = 2
 VMEM_BYTES = 60 * 1024 * 1024
 
 
@@ -187,23 +188,21 @@
     return real, jnp.concatenate([low[:, 64:], high[:, 64:]], axis=1)
 
 
-def unpack_into(ref, store):
+def unpacked(ref, channel):
     for p in range(4):
-        low = ref[pl.ds(32 * p, 16), 0].reshape(256, 128)
-        high = ref[pl.ds(32 * p + 16, 16), 0].reshape(256, 128)
-        store(pl.ds(128 * p, 128), *unpack_pair(low, high))
-
-
-def received(spectra):
-    return pl.BlockSpec((spectra.shape[0], 1, 16, 128), lambda c: (0, c, 0, 0))
+        low = ref[pl.ds(32 * p, 16), channel].reshape(256, 128)
+        high = ref[pl.ds(32 * p + 16, 16), channel].reshape(256, 128)
+        yield unpack_pair(low, high)
+
+
+def received(spectra, channels):
+    return pl.BlockSpec((spectra.shape[0], channels, 16, 128), lambda c: (0, c, 0, 0))
 
 
 def unpack_body(ref, out_ref):
-    def store(at, real, imag):
-        out_ref[0, 0, :, at] = real
-        out_ref[0, 1, :, at] = imag
-
-    unpack_into(ref, store)
+    for p, parts in enumerate(unpacked(ref, 0)):
+        for n, part in enumerate(parts):
+            out_ref[0, n, :, pl.ds(128 * p, 128)] = part
 
 
 def unpack(spectra):
@@ -211,7 +210,7 @@
     return pl.pallas_call(
         unpack_body,
         grid=(channels,),
-        in_specs=[received(spectra)],
+        in_specs=[received(spectra, 1)],
         out_specs=pl.BlockSpec((1, 2, 256, 512), lambda c: (c, 0, 0, 0)),
         out_shape=jax.ShapeDtypeStruct((channels, 2, 256, 512), jnp.bfloat16),
         compiler_params=pltpu.CompilerParams(vmem_limit_bytes=VMEM_BYTES),
@@ -221,17 +220,11 @@
     )(spectra)
 
 
-def correlate_body(scale, ready_ref, ref, out_ref, real, imag):
-    real[pl.ds(0, 256), :] = ready_ref[0, 0]
-    imag[pl.ds(0, 256), :] = ready_ref[0, 1]
-
-    def store(at, re, im):
-        real[pl.ds(256, 256), at] = re
-        imag[pl.ds(256, 256), at] = im
-
-    unpack_into(ref, store)
-    r, i = real[...], imag[...]
+def correlate_channel(scale, channel, ready_ref, ref, out_ref):
+    arrived = [jnp.concatenate(blocks, axis=1) for blocks in zip(*unpacked(ref, channel))]
+    r, i = [jnp.concatenate([ready_ref[channel, n], part], axis=0) for n, part in enumerate(arrived)]
     rt, it = r.T, i.T
+    both_t, both = jnp.concatenate([rt, it], axis=1), jnp.concatenate([r, i], axis=0)
 
     def block(left, right, m, n):
         return jnp.dot(
@@ -240,27 +233,31 @@
 
     for m, n in ((0, 0), (0, 1), (1, 1)):
         rows, columns = pl.ds(256 * m, 256), pl.ds(256 * n, 256)
-        value = (block(rt, r, m, n) + block(it, i, m, n)) * scale
+        value = block(both_t, both, m, n) * scale
         cross = block(it, r, m, n) * scale
-        out_ref[0, 0, rows, columns] = value
+        out_ref[channel, 0, rows, columns] = value
         if m == n:
-            out_ref[0, 1, rows, columns] = cross - cross.T
+            out_ref[channel, 1, rows, columns] = cross - cross.T
         else:
             cross = cross - block(rt, i, m, n) * scale
-            out_ref[0, 0, columns, rows] = value.T
-            out_ref[0, 1, rows, columns] = cross
-            out_ref[0, 1, columns, rows] = -cross.T
+            out_ref[channel, 0, columns, rows] = value.T
+            out_ref[channel, 1, rows, columns] = cross
+            out_ref[channel, 1, columns, rows] = -cross.T
+
+
+def correlate_body(scale, *refs):
+    for channel in range(CHANNEL_BLOCK):
+        correlate_channel(scale, channel, *refs)
 
 
 def correlate(first, second, frames):
     channels = second.shape[1]
     return pl.pallas_call(
         functools.partial(correlate_body, 1.0 / frames),
-        grid=(channels,),
-        in_specs=[pl.BlockSpec((1, 2, 256, 512), lambda c: (c, 0, 0, 0)), received(second)],
-        out_specs=pl.BlockSpec((1, 2, 512, 512), lambda c: (c, 0, 0, 0)),
+        grid=(channels // CHANNEL_BLOCK,),
+        in_specs=[pl.BlockSpec((CHANNEL_BLOCK, 2, 256, 512), lambda c: (c, 0, 0, 0)), received(second, CHANNEL_BLOCK)],
+        out_specs=pl.BlockSpec((CHANNEL_BLOCK, 2, 512, 512), lambda c: (c, 0, 0, 0)),
         out_shape=jax.ShapeDtypeStruct((channels, 2, 512, 512), jnp.float32),
-        scratch_shapes=[pltpu.VMEM((512, 512), jnp.bfloat16)] * 2,
         compiler_params=pltpu.CompilerParams(vmem_limit_bytes=VMEM_BYTES),
         cost_estimate=pl.CostEstimate(
             flops=16 * 512 * 512 * 1024, bytes_accessed=25 * 1024 * 1024, transcendentals=0

time: 177 us -> 175 us (0.989)
  Pallas kernels: 70 us -> 68 us
    pallas_call x1, Pallas kernels: 14.3 us -> 12.3 us  [correlate(): pl.pallas_call(functools.partial(correlate_body, 1.0 / frames), grid=(cha...]
where the time goes in v5:
time: 175 us
  waiting for transfers between devices  84.5 us (48%)
  Pallas kernels  68 us (39%)
  starting transfers between devices  21.4 us (12%)
    all_to_all x1, waiting for transfers between devices, per_device(): second = lax.all_to_all(second, AXES, 0, 0, tiled=True)  44.6 us
    pallas_call x2, Pallas kernels, channelize(): pl.pallas_call(functools.partial(channelize_body, wrap, own is None), gri...  43.2 us
    all_to_all x1, waiting for transfers between devices, per_device(): first = lax.all_to_all(first, AXES, 0, 0, tiled=True)  30.5 us
    pallas_call x1, Pallas kernels, correlate(): pl.pallas_call(functools.partial(correlate_body, 1.0 / frames), grid=(cha...  12.3 us
    ppermute x1, waiting for transfers between devices, per_device(): after = lax.ppermute(head, 'tm', down)  9.42 us
    all_to_all x1, starting transfers between devices, per_device(): first = lax.all_to_all(first, AXES, 0, 0, tiled=True)  7.69 us
    pallas_call x1, Pallas kernels, unpack(): pl.pallas_call(unpack_body, grid=(channels,), in_specs=[received(spectra,...  7.33 us
    all_to_all x1, starting transfers between devices, per_device(): second = lax.all_to_all(second, AXES, 0, 0, tiled=True)  6.04 us
  transfers between devices with their start and end apart: 4, of which 3 were waited for; matrix products, arithmetic and copies ran while one was open for 0% of the time, Pallas kernels for 30%

profile of v5, /device:TPU:7, one launch (start us, length us, event | category | flops | bytes accessed | tf_op | source)
XLA Modules:
  0.0 174.6 jit_solution(3274935779180435527)
XLA Ops:
  0.0 2.7 %shard_map.39 = bf16[64,8,16,128]{3,2,1,0:T(8,128)(2,1)} custom-call(bf16[64,32,16,128]{3,2,1,0:T(8,128)(2,1)} %bitcast.9), custom_call_target="tpu_custom_call" | custom-call | tf_op jit(solution)/shard_map/pallas_call | solution.py:176
  2.7 0.0 copy-start
  2.7 4.7 %collective-permute-start = (bf16[64,8,16,128]{3,2,1,0:T(8,128)(2,1)}, bf16[64,8,16,128]{3,2,1,0:T(8,128)(2,1)}, u32[]{:S(2)}, u32[]{:S(2)}) collective-permute-start(bf16[64,8,16,128]{3,2,1,0:T(8,128)(2,1)} %shard_map.39), channel_id=1, source_target_pairs={{0,1},{1,2},{2,3},{3,4},{4,5},{5,6},{6,7},{7,8},{8,9},{9,10},{10,1... | collective-permute-start | bytes 6291464 | tf_op jit(solution)/shard_map/ppermute | solution.py:282
  7.3 2.5 %shard_map.40 = bf16[64,7,16,128]{3,2,1,0:T(8,128)(2,1)} custom-call(bf16[64,32,16,128]{3,2,1,0:T(8,128)(2,1)} %bitcast.10), custom_call_target="tpu_custom_call" | custom-call | tf_op jit(solution)/shard_map/pallas_call | solution.py:176
  9.8 3.0 %collective-permute-start.1 = (bf16[64,7,16,128]{3,2,1,0:T(8,128)(2,1)}, bf16[64,7,16,128]{3,2,1,0:T(8,128)(2,1)}, u32[]{:S(2)}, u32[]{:S(2)}) collective-permute-start(bf16[64,7,16,128]{3,2,1,0:T(8,128)(2,1)} %shard_map.40), channel_id=1, source_target_pairs={{0,15},{1,0},{2,1},{3,2},{4,3},{5,4},{6,5},{7,6},{8,7},{9,8},{10,9... | collective-permute-start | bytes 5505032 | tf_op jit(solution)/shard_map/ppermute | solution.py:284
  12.8 0.0 copy-done
  12.8 0.7 broadcast_in_dim.3
  13.5 28.4 %shard_map.37 = (bf16[128,8,16,128]{3,2,1,0:T(8,128)(2,1)}, f32[64,16,16,128]{3,2,1,0:T(8,128)}) custom-call(f32[1]{0:T(128)} %bitcast.refs_0_, f32[16,16,128]{2,1,0:T(8,128)} %bitcast.13, bf16[4,256,512]{2,1,0:T(8,128)(2,1)} %constant.8.clone.refs_2_.refs_1_, bf16[64,32,16,128]{3,2,1,0:T(8,128)(2,1)} %bitcast.11), custom_call_target="tpu_custom_call" | custom-call | flops 274877906944 | bytes 17825792 | tf_op jit(solution)/shard_map/pallas_call | solution.py:151
  41.9 7.7 %all-to-all-start = ((bf16[128,8,16,128]{3,2,1,0:T(8,128)(2,1)}), bf16[128,8,16,128]{3,2,1,0:T(8,128)(2,1)}, u32[]{:S(2)}, u32[]{:S(2)}) async-start(bf16[128,8,16,128]{3,2,1,0:T(8,128)(2,1)} %get-tuple-element.8), calls=%async_computation | async-start | bytes 8388608 | tf_op jit(solution)/shard_map/all_to_all | solution.py:292
  49.6 9.4 %collective-permute-done.1.refs_4_ = bf16[64,7,16,128]{3,2,1,0:T(8,128)(2,1)} collective-permute-done((bf16[64,7,16,128]{3,2,1,0:T(8,128)(2,1)}, bf16[64,7,16,128]{3,2,1,0:T(8,128)(2,1)}, u32[]{:S(2)}, u32[]{:S(2)}) %collective-permute-start.1) | collective-permute-done | bytes 1835040 | tf_op jit(solution)/shard_map/ppermute | solution.py:284
  59.1 0.0 collective-permute-done.refs_3_
  59.1 14.8 %shard_map.41 = bf16[128,8,16,128]{3,2,1,0:T(8,128)(2,1)} custom-call(f32[16,16,128]{2,1,0:T(8,128)} %bitcast.14, bf16[4,256,512]{2,1,0:T(8,128)(2,1)} %constant.8.clone.refs_2_.refs_1_, f32[64,16,16,128]{3,2,1,0:T(8,128)} %get-tuple-element.9.refs_2_, bf16[64,8,16,128]{3,2,1,0:T(8,128)(2,1)} %collective-permute-done.refs_3_, ...), custom_call_target="tpu_custom_call" | custom-call | flops 274877906944 | bytes 17825792 | tf_op jit(solution)/shard_map/pallas_call | solution.py:151
  73.8 30.5 %all-to-all-done.ref = bf16[128,8,16,128]{3,2,1,0:T(8,128)(2,1)} async-done(((bf16[128,8,16,128]{3,2,1,0:T(8,128)(2,1)}), bf16[128,8,16,128]{3,2,1,0:T(8,128)(2,1)}, u32[]{:S(2)}, u32[]{:S(2)}) %all-to-all-start) | async-done | bytes 4194336 | tf_op jit(solution)/shard_map/all_to_all | solution.py:292
  104.3 6.0 %all-to-all-start.1 = ((bf16[128,8,16,128]{3,2,1,0:T(8,128)(2,1)}), bf16[128,8,16,128]{3,2,1,0:T(8,128)(2,1)}, u32[]{:S(2)}, u32[]{:S(2)}) async-start(bf16[128,8,16,128]{3,2,1,0:T(8,128)(2,1)} %shard_map.41), calls=%async_computation.1 | async-start | bytes 8388608 | tf_op jit(solution)/shard_map/all_to_all | solution.py:293
  110.4 7.3 %shard_map.38.refs_0_ = bf16[8,2,256,512]{3,2,1,0:T(8,128)(2,1)} custom-call(bf16[128,8,16,128]{3,2,1,0:T(8,128)(2,1)} %all-to-all-done.ref), custom_call_target="tpu_custom_call" | custom-call | flops 274877906944 | bytes 9437184 | tf_op jit(solution)/shard_map/pallas_call | solution.py:210
  117.7 44.6 %all-to-all-done.1.refs_1_ = bf16[128,8,16,128]{3,2,1,0:T(8,128)(2,1)} async-done(((bf16[128,8,16,128]{3,2,1,0:T(8,128)(2,1)}), bf16[128,8,16,128]{3,2,1,0:T(8,128)(2,1)}, u32[]{:S(2)}, u32[]{:S(2)}) %all-to-all-start.1) | async-done | bytes 4194336 | tf_op jit(solution)/shard_map/all_to_all | solution.py:293
  162.3 12.3 %shard_map.42 = f32[8,2,512,512]{3,2,1,0:T(8,128)} custom-call(bf16[8,2,256,512]{3,2,1,0:T(8,128)(2,1)} %shard_map.38.refs_0_, bf16[128,8,16,128]{3,2,1,0:T(8,128)(2,1)} %all-to-all-done.1.refs_1_), custom_call_target="tpu_custom_call" | custom-call | flops 4294967296 | bytes 26214400 | tf_op jit(solution)/shard_map/pallas_call | solution.py:255
  (1 shorter events, 0.0 us)
Async XLA Ops:
  2.7 10.2 %copy-start = (f32[16,1024]{1,0:T(8,128)S(1)}, f32[16,1024]{1,0:T(8,128)}, u32[]{:S(2)}) copy-start(f32[16,1024]{1,0:T(8,128)} %param.4) | copy-start | bytes 196612
  2.7 56.4 %collective-permute-start = (bf16[64,8,16,128]{3,2,1,0:T(8,128)(2,1)}, bf16[64,8,16,128]{3,2,1,0:T(8,128)(2,1)}, u32[]{:S(2)}, u32[]{:S(2)}) collective-permute-start(bf16[64,8,16,128]{3,2,1,0:T(8,128)(2,1)} %shard_map.39), channel_id=1, source_target_pairs={{0,1},{1,2},{2,3},{3,4},{4,5},{5,6},{6,7},{7,8},{8,9},{9,10},{10,1... | collective-permute-start | bytes 6291464 | tf_op jit(solution)/shard_map/ppermute | solution.py:282
  9.8 49.2 %collective-permute-start.1 = (bf16[64,7,16,128]{3,2,1,0:T(8,128)(2,1)}, bf16[64,7,16,128]{3,2,1,0:T(8,128)(2,1)}, u32[]{:S(2)}, u32[]{:S(2)}) collective-permute-start(bf16[64,7,16,128]{3,2,1,0:T(8,128)(2,1)} %shard_map.40), channel_id=1, source_target_pairs={{0,15},{1,0},{2,1},{3,2},{4,3},{5,4},{6,5},{7,6},{8,7},{9,8},{10,9... | collective-permute-start | bytes 5505032 | tf_op jit(solution)/shard_map/ppermute | solution.py:284
  41.9 62.4 %all-to-all-start = ((bf16[128,8,16,128]{3,2,1,0:T(8,128)(2,1)}), bf16[128,8,16,128]{3,2,1,0:T(8,128)(2,1)}, u32[]{:S(2)}, u32[]{:S(2)}) async-start(bf16[128,8,16,128]{3,2,1,0:T(8,128)(2,1)} %get-tuple-element.8), calls=%async_computation | async-start | bytes 8388608 | tf_op jit(solution)/shard_map/all_to_all | solution.py:292
  104.3 58.0 %all-to-all-start.1 = ((bf16[128,8,16,128]{3,2,1,0:T(8,128)(2,1)}), bf16[128,8,16,128]{3,2,1,0:T(8,128)(2,1)}, u32[]{:S(2)}, u32[]{:S(2)}) async-start(bf16[128,8,16,128]{3,2,1,0:T(8,128)(2,1)} %shard_map.41), calls=%async_computation.1 | async-start | bytes 8388608 | tf_op jit(solution)/shard_map/all_to_all | solution.py:293

commit v6 on v5

--- a/solution.py
+++ b/solution.py
@@ -66,15 +66,22 @@
     step = pl.program_id(0)
     rows = INPUT_BLOCK
     if halo:
-        taps_ref, table_ref, partial_ref, before_ref, after_ref, out_ref, filtered, data, turned = refs
+        taps_ref, table_ref, partial_ref, before_ref, after_ref, out_ref, filtered, data, turned, taps_rows = refs
     else:
-        keep_ref, taps_ref, table_ref, own_ref, out_ref, partial_ref, filtered, data, turned = refs
+        keep_ref, taps_ref, table_ref, own_ref, out_ref, partial_ref, filtered, data, turned, taps_rows = refs
+
+    @pl.when(step == 0)
+    def _():
+        for j in range(8):
+            block = taps_ref[:, 128 * j : 128 * j + 128]
+            for part in range(2):
+                taps_rows[:, 2 * j + part, :] = block
 
     def filter_input(i, _):
         if halo:
-            filter_halo(i, wrap, taps_ref, partial_ref, before_ref, after_ref, filtered)
+            filter_halo(i, wrap, taps_rows, partial_ref, before_ref, after_ref, filtered)
         else:
-            filter_own(i, wrap, keep_ref[0], taps_ref, own_ref, partial_ref, filtered)
+            filter_own(i, wrap, keep_ref[0], taps_rows, own_ref, partial_ref, filtered)
         return 0
 
     lax.fori_loop(0, rows, filter_input, 0)
@@ -119,7 +126,7 @@
                 turned[pl.ds(256 * TURN * p + 2 * n + 1, 256, stride=TURN), :] = result[:, 128:]
             return 0
 
-        lax.fori_loop(0, 8, transform, 0)
+        lax.fori_loop(0, 8, transform, 0, unroll=2)
 
         def write(d, _):
             for q in range(2):
@@ -158,6 +165,7 @@
             pltpu.VMEM((16, INPUT_BLOCK * PITCH, 128), jnp.float32),
             pltpu.VMEM((4, 16, 2, 64, 512), jnp.bfloat16),
             pltpu.VMEM((1024 * TURN, 128), jnp.float32),
+            pltpu.VMEM((taps.shape[0], 16, 128), jnp.float32),
         ],
         compiler_params=pltpu.CompilerParams(vmem_limit_bytes=VMEM_BYTES),
         cost_estimate=pl.CostEstimate(
@@ -282,13 +290,12 @@
     before = lax.ppermute(tail, "tm", up)
     head = edge(lax.optimization_barrier((own, tail))[0], 0, 0, after_count)
     after = lax.ppermute(head, "tm", down)
-    taps_rows = jnp.repeat(taps.reshape(tap_count, 8, 1, 128), 2, axis=2).reshape(tap_count, 16, 128)
     table = jnp.asarray(transform_rows(nfft))
     keep = (lax.axis_index("tm") < n_tm - 1).astype(jnp.float32).reshape(1)
 
     wrap = BEFORE + frames
-    first, partial = channelize(taps_rows, table, devices, wrap, own=own, keep=keep)
-    second = channelize(taps_rows, table, devices, wrap, partial=partial, halo=(before, after))
+    first, partial = channelize(taps, table, devices, wrap, own=own, keep=keep)
+    second = channelize(taps, table, devices, wrap, partial=partial, halo=(before, after))
     first = lax.all_to_all(first, AXES, 0, 0, tiled=True)
     second = lax.all_to_all(second, AXES, 0, 0, tiled=True)
     return correlate(unpack(first), second, n_tm * frames)

time: 175 us -> 181 us (1.034)
  starting transfers between devices: 21.4 us -> 26.7 us
  waiting for transfers between devices: 84.5 us -> 87.5 us
    all_to_all x1, starting transfers between devices: 6.04 us -> 11.5 us  [per_device(): second = lax.all_to_all(second, AXES, 0, 0, tiled=True)]
    ppermute x1, waiting for transfers between devices: 9.42 us -> 12.5 us  [per_device(): after = lax.ppermute(head, 'tm', down)]
  transfers between devices with their start and end apart: 4 -> 4, of which waited for: 3 -> 3; matrix products, arithmetic and copies ran while one was open for 0% -> 0% of each run, Pallas kernels for 30% -> 28%
where the time goes in v6:
time: 181 us
  waiting for transfers between devices  87.5 us (48%)
  Pallas kernels  66.3 us (37%)
  starting transfers between devices  26.7 us (15%)
    all_to_all x1, waiting for transfers between devices, per_device(): second = lax.all_to_all(second, AXES, 0, 0, tiled=True)  44.6 us
    pallas_call x2, Pallas kernels, channelize(): pl.pallas_call(functools.partial(channelize_body, wrap, own is None), gri...  41.5 us
    all_to_all x1, waiting for transfers between devices, per_device(): first = lax.all_to_all(first, AXES, 0, 0, tiled=True)  30.4 us
    ppermute x1, waiting for transfers between devices, per_device(): after = lax.ppermute(head, 'tm', down)  12.5 us
    pallas_call x1, Pallas kernels, correlate(): pl.pallas_call(functools.partial(correlate_body, 1.0 / frames), grid=(cha...  12.3 us
    all_to_all x1, starting transfers between devices, per_device(): second = lax.all_to_all(second, AXES, 0, 0, tiled=True)  11.5 us
    all_to_all x1, starting transfers between devices, per_device(): first = lax.all_to_all(first, AXES, 0, 0, tiled=True)  7.68 us
    pallas_call x1, Pallas kernels, unpack(): pl.pallas_call(unpack_body, grid=(channels,), in_specs=[received(spectra,...  7.36 us
  transfers between devices with their start and end apart: 4, of which 3 were waited for; matrix products, arithmetic and copies ran while one was open for 0% of the time, Pallas kernels for 28%

profile of v6, /device:TPU:7, one launch (start us, length us, event | category | flops | bytes accessed | tf_op | source)
XLA Modules:
  0.0 180.5 jit_solution(13994578855512579819)
XLA Ops:
  0.0 2.7 %shard_map.39 = bf16[64,8,16,128]{3,2,1,0:T(8,128)(2,1)} custom-call(bf16[64,32,16,128]{3,2,1,0:T(8,128)(2,1)} %bitcast.6), custom_call_target="tpu_custom_call" | custom-call | tf_op jit(solution)/shard_map/pallas_call | solution.py:184
  2.7 4.5 %collective-permute-start = (bf16[64,8,16,128]{3,2,1,0:T(8,128)(2,1)}, bf16[64,8,16,128]{3,2,1,0:T(8,128)(2,1)}, u32[]{:S(2)}, u32[]{:S(2)}) collective-permute-start(bf16[64,8,16,128]{3,2,1,0:T(8,128)(2,1)} %shard_map.39), channel_id=1, source_target_pairs={{0,1},{1,2},{2,3},{3,4},{4,5},{5,6},{6,7},{7,8},{8,9},{9,10},{10,1... | collective-permute-start | bytes 6291464 | tf_op jit(solution)/shard_map/ppermute | solution.py:290
  7.2 2.5 %shard_map.40 = bf16[64,7,16,128]{3,2,1,0:T(8,128)(2,1)} custom-call(bf16[64,32,16,128]{3,2,1,0:T(8,128)(2,1)} %bitcast.7), custom_call_target="tpu_custom_call" | custom-call | tf_op jit(solution)/shard_map/pallas_call | solution.py:184
  9.7 3.0 %collective-permute-start.1 = (bf16[64,7,16,128]{3,2,1,0:T(8,128)(2,1)}, bf16[64,7,16,128]{3,2,1,0:T(8,128)(2,1)}, u32[]{:S(2)}, u32[]{:S(2)}) collective-permute-start(bf16[64,7,16,128]{3,2,1,0:T(8,128)(2,1)} %shard_map.40), channel_id=1, source_target_pairs={{0,15},{1,0},{2,1},{3,2},{4,3},{5,4},{6,5},{7,6},{8,7},{9,8},{10,9... | collective-permute-start | bytes 5505032 | tf_op jit(solution)/shard_map/ppermute | solution.py:292
  12.7 27.3 %shard_map.37 = (bf16[128,8,16,128]{3,2,1,0:T(8,128)(2,1)}, f32[64,16,16,128]{3,2,1,0:T(8,128)}) custom-call(f32[1]{0:T(128)} %bitcast.refs_0_, f32[16,1024]{1,0:T(8,128)} %refs_0_.1, bf16[4,256,512]{2,1,0:T(8,128)(2,1)} %constant.8.clone.refs_2_.refs_1_, bf16[64,32,16,128]{3,2,1,0:T(8,128)(2,1)} %bitcast.8), custom_call_target="tpu_custom_call" | custom-call | flops 274877906944 | bytes 17825792 | tf_op jit(solution)/shard_map/pallas_call | solution.py:158
  40.0 7.7 %all-to-all-start = ((bf16[128,8,16,128]{3,2,1,0:T(8,128)(2,1)}), bf16[128,8,16,128]{3,2,1,0:T(8,128)(2,1)}, u32[]{:S(2)}, u32[]{:S(2)}) async-start(bf16[128,8,16,128]{3,2,1,0:T(8,128)(2,1)} %get-tuple-element.8), calls=%async_computation | async-start | bytes 8388608 | tf_op jit(solution)/shard_map/all_to_all | solution.py:299
  47.7 12.5 %collective-permute-done.1.refs_4_ = bf16[64,7,16,128]{3,2,1,0:T(8,128)(2,1)} collective-permute-done((bf16[64,7,16,128]{3,2,1,0:T(8,128)(2,1)}, bf16[64,7,16,128]{3,2,1,0:T(8,128)(2,1)}, u32[]{:S(2)}, u32[]{:S(2)}) %collective-permute-start.1) | collective-permute-done | bytes 1835040 | tf_op jit(solution)/shard_map/ppermute | solution.py:292
  60.2 0.0 collective-permute-done.refs_3_
  60.2 14.2 %shard_map.41 = bf16[128,8,16,128]{3,2,1,0:T(8,128)(2,1)} custom-call(f32[16,1024]{1,0:T(8,128)} %refs_0_.1, bf16[4,256,512]{2,1,0:T(8,128)(2,1)} %constant.8.clone.refs_2_.refs_1_, f32[64,16,16,128]{3,2,1,0:T(8,128)} %get-tuple-element.9.refs_2_, bf16[64,8,16,128]{3,2,1,0:T(8,128)(2,1)} %collective-permute-done.refs_3_, ...), custom_call_target="tpu_custom_call" | custom-call | flops 274877906944 | bytes 17825792 | tf_op jit(solution)/shard_map/pallas_call | solution.py:158
  74.4 30.4 %all-to-all-done.ref = bf16[128,8,16,128]{3,2,1,0:T(8,128)(2,1)} async-done(((bf16[128,8,16,128]{3,2,1,0:T(8,128)(2,1)}), bf16[128,8,16,128]{3,2,1,0:T(8,128)(2,1)}, u32[]{:S(2)}, u32[]{:S(2)}) %all-to-all-start) | async-done | bytes 4194336 | tf_op jit(solution)/shard_map/all_to_all | solution.py:299
  104.8 11.5 %all-to-all-start.1 = ((bf16[128,8,16,128]{3,2,1,0:T(8,128)(2,1)}), bf16[128,8,16,128]{3,2,1,0:T(8,128)(2,1)}, u32[]{:S(2)}, u32[]{:S(2)}) async-start(bf16[128,8,16,128]{3,2,1,0:T(8,128)(2,1)} %shard_map.41), calls=%async_computation.1 | async-start | bytes 8388608 | tf_op jit(solution)/shard_map/all_to_all | solution.py:300
  116.3 7.4 %shard_map.38.refs_0_ = bf16[8,2,256,512]{3,2,1,0:T(8,128)(2,1)} custom-call(bf16[128,8,16,128]{3,2,1,0:T(8,128)(2,1)} %all-to-all-done.ref), custom_call_target="tpu_custom_call" | custom-call | flops 274877906944 | bytes 9437184 | tf_op jit(solution)/shard_map/pallas_call | solution.py:218
  123.7 44.6 %all-to-all-done.1.refs_1_ = bf16[128,8,16,128]{3,2,1,0:T(8,128)(2,1)} async-done(((bf16[128,8,16,128]{3,2,1,0:T(8,128)(2,1)}), bf16[128,8,16,128]{3,2,1,0:T(8,128)(2,1)}, u32[]{:S(2)}, u32[]{:S(2)}) %all-to-all-start.1) | async-done | bytes 4194336 | tf_op jit(solution)/shard_map/all_to_all | solution.py:300
  168.2 12.3 %shard_map.42 = f32[8,2,512,512]{3,2,1,0:T(8,128)} custom-call(bf16[8,2,256,512]{3,2,1,0:T(8,128)(2,1)} %shard_map.38.refs_0_, bf16[128,8,16,128]{3,2,1,0:T(8,128)(2,1)} %all-to-all-done.1.refs_1_), custom_call_target="tpu_custom_call" | custom-call | flops 4294967296 | bytes 26214400 | tf_op jit(solution)/shard_map/pallas_call | solution.py:263
Async XLA Ops:
  2.7 57.5 %collective-permute-start = (bf16[64,8,16,128]{3,2,1,0:T(8,128)(2,1)}, bf16[64,8,16,128]{3,2,1,0:T(8,128)(2,1)}, u32[]{:S(2)}, u32[]{:S(2)}) collective-permute-start(bf16[64,8,16,128]{3,2,1,0:T(8,128)(2,1)} %shard_map.39), channel_id=1, source_target_pairs={{0,1},{1,2},{2,3},{3,4},{4,5},{5,6},{6,7},{7,8},{8,9},{9,10},{10,1... | collective-permute-start | bytes 6291464 | tf_op jit(solution)/shard_map/ppermute | solution.py:290
  9.7 50.5 %collective-permute-start.1 = (bf16[64,7,16,128]{3,2,1,0:T(8,128)(2,1)}, bf16[64,7,16,128]{3,2,1,0:T(8,128)(2,1)}, u32[]{:S(2)}, u32[]{:S(2)}) collective-permute-start(bf16[64,7,16,128]{3,2,1,0:T(8,128)(2,1)} %shard_map.40), channel_id=1, source_target_pairs={{0,15},{1,0},{2,1},{3,2},{4,3},{5,4},{6,5},{7,6},{8,7},{9,8},{10,9... | collective-permute-start | bytes 5505032 | tf_op jit(solution)/shard_map/ppermute | solution.py:292
  40.0 64.8 %all-to-all-start = ((bf16[128,8,16,128]{3,2,1,0:T(8,128)(2,1)}), bf16[128,8,16,128]{3,2,1,0:T(8,128)(2,1)}, u32[]{:S(2)}, u32[]{:S(2)}) async-start(bf16[128,8,16,128]{3,2,1,0:T(8,128)(2,1)} %get-tuple-element.8), calls=%async_computation | async-start | bytes 8388608 | tf_op jit(solution)/shard_map/all_to_all | solution.py:299
  104.8 63.4 %all-to-all-start.1 = ((bf16[128,8,16,128]{3,2,1,0:T(8,128)(2,1)}), bf16[128,8,16,128]{3,2,1,0:T(8,128)(2,1)}, u32[]{:S(2)}, u32[]{:S(2)}) async-start(bf16[128,8,16,128]{3,2,1,0:T(8,128)(2,1)} %shard_map.41), calls=%async_computation.1 | async-start | bytes 8388608 | tf_op jit(solution)/shard_map/all_to_all | solution.py:300

commit v7 on v5

--- a/solution.py
+++ b/solution.py
@@ -155,9 +155,9 @@
         out_specs=out_specs,
         out_shape=out_shape,
         scratch_shapes=[
-            pltpu.VMEM((16, INPUT_BLOCK * PITCH, 128), jnp.float32),
+            pltpu.VMEM((16, INPUT_BLOCK * PITCH + 16, 128), jnp.float32),
             pltpu.VMEM((4, 16, 2, 64, 512), jnp.bfloat16),
-            pltpu.VMEM((1024 * TURN, 128), jnp.float32),
+            pltpu.VMEM((1024 * TURN + 16, 128), jnp.float32),
         ],
         compiler_params=pltpu.CompilerParams(vmem_limit_bytes=VMEM_BYTES),
         cost_estimate=pl.CostEstimate(

time: 175 us -> 176 us (level)
  transfers between devices with their start and end apart: 4 -> 4, of which waited for: 3 -> 3; matrix products, arithmetic and copies ran while one was open for 0% -> 0% of each run, Pallas kernels for 30% -> 31%
where the time goes in v7:
time: 176 us; the launch traced here: 175 us
  waiting for transfers between devices  83.5 us (47%)
  Pallas kernels  68.8 us (39%)
  starting transfers between devices  22.5 us (13%)
    all_to_all x1, waiting for transfers between devices, per_device(): second = lax.all_to_all(second, AXES, 0, 0, tiled=True)  44.7 us
    pallas_call x2, Pallas kernels, channelize(): pl.pallas_call(functools.partial(channelize_body, wrap, own is None), gri...  44 us
    all_to_all x1, waiting for transfers between devices, per_device(): first = lax.all_to_all(first, AXES, 0, 0, tiled=True)  30.9 us
    pallas_call x1, Pallas kernels, correlate(): pl.pallas_call(functools.partial(correlate_body, 1.0 / frames), grid=(cha...  12.3 us
    ppermute x1, waiting for transfers between devices, per_device(): after = lax.ppermute(head, 'tm', down)  7.82 us
    all_to_all x1, starting transfers between devices, per_device(): first = lax.all_to_all(first, AXES, 0, 0, tiled=True)  7.69 us
    pallas_call x1, Pallas kernels, unpack(): pl.pallas_call(unpack_body, grid=(channels,), in_specs=[received(spectra,...  7.33 us
    all_to_all x1, starting transfers between devices, per_device(): second = lax.all_to_all(second, AXES, 0, 0, tiled=True)  7.19 us
  transfers between devices with their start and end apart: 4, of which 3 were waited for; matrix products, arithmetic and copies ran while one was open for 0% of the time, Pallas kernels for 31%

profile of v7, /device:TPU:7, one launch (start us, length us, event | category | flops | bytes accessed | tf_op | source)
XLA Modules:
  0.0 175.5 jit_solution(406862760649545080)
XLA Ops:
  0.0 2.7 %shard_map.39 = bf16[64,8,16,128]{3,2,1,0:T(8,128)(2,1)} custom-call(bf16[64,32,16,128]{3,2,1,0:T(8,128)(2,1)} %bitcast.9), custom_call_target="tpu_custom_call" | custom-call | tf_op jit(solution)/shard_map/pallas_call | solution.py:176
  2.7 0.0 copy-start
  2.7 4.7 %collective-permute-start = (bf16[64,8,16,128]{3,2,1,0:T(8,128)(2,1)}, bf16[64,8,16,128]{3,2,1,0:T(8,128)(2,1)}, u32[]{:S(2)}, u32[]{:S(2)}) collective-permute-start(bf16[64,8,16,128]{3,2,1,0:T(8,128)(2,1)} %shard_map.39), channel_id=1, source_target_pairs={{0,1},{1,2},{2,3},{3,4},{4,5},{5,6},{6,7},{7,8},{8,9},{9,10},{10,1... | collective-permute-start | bytes 6291464 | tf_op jit(solution)/shard_map/ppermute | solution.py:282
  7.3 2.5 %shard_map.40 = bf16[64,7,16,128]{3,2,1,0:T(8,128)(2,1)} custom-call(bf16[64,32,16,128]{3,2,1,0:T(8,128)(2,1)} %bitcast.10), custom_call_target="tpu_custom_call" | custom-call | tf_op jit(solution)/shard_map/pallas_call | solution.py:176
  9.8 3.0 %collective-permute-start.1 = (bf16[64,7,16,128]{3,2,1,0:T(8,128)(2,1)}, bf16[64,7,16,128]{3,2,1,0:T(8,128)(2,1)}, u32[]{:S(2)}, u32[]{:S(2)}) collective-permute-start(bf16[64,7,16,128]{3,2,1,0:T(8,128)(2,1)} %shard_map.40), channel_id=1, source_target_pairs={{0,15},{1,0},{2,1},{3,2},{4,3},{5,4},{6,5},{7,6},{8,7},{9,8},{10,9... | collective-permute-start | bytes 5505032 | tf_op jit(solution)/shard_map/ppermute | solution.py:284
  12.8 0.0 copy-done
  12.8 0.7 broadcast_in_dim.3
  13.5 29.2 %shard_map.37 = (bf16[128,8,16,128]{3,2,1,0:T(8,128)(2,1)}, f32[64,16,16,128]{3,2,1,0:T(8,128)}) custom-call(f32[1]{0:T(128)} %bitcast.refs_0_, f32[16,16,128]{2,1,0:T(8,128)} %bitcast.13, bf16[4,256,512]{2,1,0:T(8,128)(2,1)} %constant.8.clone.refs_2_.refs_1_, bf16[64,32,16,128]{3,2,1,0:T(8,128)(2,1)} %bitcast.11), custom_call_target="tpu_custom_call" | custom-call | flops 274877906944 | bytes 17825792 | tf_op jit(solution)/shard_map/pallas_call | solution.py:151
  42.7 7.7 %all-to-all-start = ((bf16[128,8,16,128]{3,2,1,0:T(8,128)(2,1)}), bf16[128,8,16,128]{3,2,1,0:T(8,128)(2,1)}, u32[]{:S(2)}, u32[]{:S(2)}) async-start(bf16[128,8,16,128]{3,2,1,0:T(8,128)(2,1)} %get-tuple-element.8), calls=%async_computation | async-start | bytes 8388608 | tf_op jit(solution)/shard_map/all_to_all | solution.py:292
  50.4 7.8 %collective-permute-done.1.refs_4_ = bf16[64,7,16,128]{3,2,1,0:T(8,128)(2,1)} collective-permute-done((bf16[64,7,16,128]{3,2,1,0:T(8,128)(2,1)}, bf16[64,7,16,128]{3,2,1,0:T(8,128)(2,1)}, u32[]{:S(2)}, u32[]{:S(2)}) %collective-permute-start.1) | collective-permute-done | bytes 1835040 | tf_op jit(solution)/shard_map/ppermute | solution.py:284
  58.2 0.0 collective-permute-done.refs_3_
  58.2 14.8 %shard_map.41 = bf16[128,8,16,128]{3,2,1,0:T(8,128)(2,1)} custom-call(f32[16,16,128]{2,1,0:T(8,128)} %bitcast.14, bf16[4,256,512]{2,1,0:T(8,128)(2,1)} %constant.8.clone.refs_2_.refs_1_, f32[64,16,16,128]{3,2,1,0:T(8,128)} %get-tuple-element.9.refs_2_, bf16[64,8,16,128]{3,2,1,0:T(8,128)(2,1)} %collective-permute-done.refs_3_, ...), custom_call_target="tpu_custom_call" | custom-call | flops 274877906944 | bytes 17825792 | tf_op jit(solution)/shard_map/pallas_call | solution.py:151
  73.0 30.9 %all-to-all-done.ref = bf16[128,8,16,128]{3,2,1,0:T(8,128)(2,1)} async-done(((bf16[128,8,16,128]{3,2,1,0:T(8,128)(2,1)}), bf16[128,8,16,128]{3,2,1,0:T(8,128)(2,1)}, u32[]{:S(2)}, u32[]{:S(2)}) %all-to-all-start) | async-done | bytes 4194336 | tf_op jit(solution)/shard_map/all_to_all | solution.py:292
  104.0 7.2 %all-to-all-start.1 = ((bf16[128,8,16,128]{3,2,1,0:T(8,128)(2,1)}), bf16[128,8,16,128]{3,2,1,0:T(8,128)(2,1)}, u32[]{:S(2)}, u32[]{:S(2)}) async-start(bf16[128,8,16,128]{3,2,1,0:T(8,128)(2,1)} %shard_map.41), calls=%async_computation.1 | async-start | bytes 8388608 | tf_op jit(solution)/shard_map/all_to_all | solution.py:293
  111.2 7.3 %shard_map.38.refs_0_ = bf16[8,2,256,512]{3,2,1,0:T(8,128)(2,1)} custom-call(bf16[128,8,16,128]{3,2,1,0:T(8,128)(2,1)} %all-to-all-done.ref), custom_call_target="tpu_custom_call" | custom-call | flops 274877906944 | bytes 9437184 | tf_op jit(solution)/shard_map/pallas_call | solution.py:210
  118.5 44.7 %all-to-all-done.1.refs_1_ = bf16[128,8,16,128]{3,2,1,0:T(8,128)(2,1)} async-done(((bf16[128,8,16,128]{3,2,1,0:T(8,128)(2,1)}), bf16[128,8,16,128]{3,2,1,0:T(8,128)(2,1)}, u32[]{:S(2)}, u32[]{:S(2)}) %all-to-all-start.1) | async-done | bytes 4194336 | tf_op jit(solution)/shard_map/all_to_all | solution.py:293
  163.2 12.3 %shard_map.42 = f32[8,2,512,512]{3,2,1,0:T(8,128)} custom-call(bf16[8,2,256,512]{3,2,1,0:T(8,128)(2,1)} %shard_map.38.refs_0_, bf16[128,8,16,128]{3,2,1,0:T(8,128)(2,1)} %all-to-all-done.1.refs_1_), custom_call_target="tpu_custom_call" | custom-call | flops 4294967296 | bytes 26214400 | tf_op jit(solution)/shard_map/pallas_call | solution.py:255
  (1 shorter events, 0.0 us)
Async XLA Ops:
  2.7 10.2 %copy-start = (f32[16,1024]{1,0:T(8,128)S(1)}, f32[16,1024]{1,0:T(8,128)}, u32[]{:S(2)}) copy-start(f32[16,1024]{1,0:T(8,128)} %param.4) | copy-start | bytes 196612
  2.7 55.6 %collective-permute-start = (bf16[64,8,16,128]{3,2,1,0:T(8,128)(2,1)}, bf16[64,8,16,128]{3,2,1,0:T(8,128)(2,1)}, u32[]{:S(2)}, u32[]{:S(2)}) collective-permute-start(bf16[64,8,16,128]{3,2,1,0:T(8,128)(2,1)} %shard_map.39), channel_id=1, source_target_pairs={{0,1},{1,2},{2,3},{3,4},{4,5},{5,6},{6,7},{7,8},{8,9},{9,10},{10,1... | collective-permute-start | bytes 6291464 | tf_op jit(solution)/shard_map/ppermute | solution.py:282
  9.8 48.4 %collective-permute-start.1 = (bf16[64,7,16,128]{3,2,1,0:T(8,128)(2,1)}, bf16[64,7,16,128]{3,2,1,0:T(8,128)(2,1)}, u32[]{:S(2)}, u32[]{:S(2)}) collective-permute-start(bf16[64,7,16,128]{3,2,1,0:T(8,128)(2,1)} %shard_map.40), channel_id=1, source_target_pairs={{0,15},{1,0},{2,1},{3,2},{4,3},{5,4},{6,5},{7,6},{8,7},{9,8},{10,9... | collective-permute-start | bytes 5505032 | tf_op jit(solution)/shard_map/ppermute | solution.py:284
  42.7 61.3 %all-to-all-start = ((bf16[128,8,16,128]{3,2,1,0:T(8,128)(2,1)}), bf16[128,8,16,128]{3,2,1,0:T(8,128)(2,1)}, u32[]{:S(2)}, u32[]{:S(2)}) async-start(bf16[128,8,16,128]{3,2,1,0:T(8,128)(2,1)} %get-tuple-element.8), calls=%async_computation | async-start | bytes 8388608 | tf_op jit(solution)/shard_map/all_to_all | solution.py:292
  104.0 59.2 %all-to-all-start.1 = ((bf16[128,8,16,128]{3,2,1,0:T(8,128)(2,1)}), bf16[128,8,16,128]{3,2,1,0:T(8,128)(2,1)}, u32[]{:S(2)}, u32[]{:S(2)}) async-start(bf16[128,8,16,128]{3,2,1,0:T(8,128)(2,1)} %shard_map.41), calls=%async_computation.1 | async-start | bytes 8388608 | tf_op jit(solution)/shard_map/all_to_all | solution.py:293

commit v8 on v6

--- a/solution.py
+++ b/solution.py
@@ -126,7 +126,7 @@
                 turned[pl.ds(256 * TURN * p + 2 * n + 1, 256, stride=TURN), :] = result[:, 128:]
             return 0
 
-        lax.fori_loop(0, 8, transform, 0, unroll=2)
+        lax.fori_loop(0, 8, transform, 0, unroll=2 if halo else 1)
 
         def write(d, _):
             for q in range(2):
@@ -162,9 +162,9 @@
         out_specs=out_specs,
         out_shape=out_shape,
         scratch_shapes=[
-            pltpu.VMEM((16, INPUT_BLOCK * PITCH, 128), jnp.float32),
+            pltpu.VMEM((16, INPUT_BLOCK * PITCH + 16, 128), jnp.float32),
             pltpu.VMEM((4, 16, 2, 64, 512), jnp.bfloat16),
-            pltpu.VMEM((1024 * TURN, 128), jnp.float32),
+            pltpu.VMEM((1024 * TURN + 16, 128), jnp.float32),
             pltpu.VMEM((taps.shape[0], 16, 128), jnp.float32),
         ],
         compiler_params=pltpu.CompilerParams(vmem_limit_bytes=VMEM_BYTES),

time: 181 us -> 176 us (0.972)
  starting transfers between devices: 26.7 us -> 21.8 us
  waiting for transfers between devices: 87.5 us -> 85.6 us
    all_to_all x1, starting transfers between devices: 11.5 us -> 6.61 us  [per_device(): second = lax.all_to_all(second, AXES, 0, 0, tiled=True)]
    ppermute x1, waiting for transfers between devices: 12.5 us -> 9.83 us  [per_device(): after = lax.ppermute(head, 'tm', down)]
  transfers between devices with their start and end apart: 4 -> 4, of which waited for: 3 -> 3; matrix products, arithmetic and copies ran while one was open for 0% -> 0% of each run, Pallas kernels for 28% -> 30%
where the time goes in v8:
time: 176 us; the launch traced here: 175 us
  waiting for transfers between devices  85.6 us (49%)
  Pallas kernels  67.8 us (39%)
  starting transfers between devices  21.8 us (12%)
    all_to_all x1, waiting for transfers between devices, per_device(): second = lax.all_to_all(second, AXES, 0, 0, tiled=True)  44.6 us
    pallas_call x2, Pallas kernels, channelize(): pl.pallas_call(functools.partial(channelize_body, wrap, own is None), gri...  42.9 us
    all_to_all x1, waiting for transfers between devices, per_device(): first = lax.all_to_all(first, AXES, 0, 0, tiled=True)  31.2 us
    pallas_call x1, Pallas kernels, correlate(): pl.pallas_call(functools.partial(correlate_body, 1.0 / frames), grid=(cha...  12.3 us
    ppermute x1, waiting for transfers between devices, per_device(): after = lax.ppermute(head, 'tm', down)  9.83 us
    all_to_all x1, starting transfers between devices, per_device(): first = lax.all_to_all(first, AXES, 0, 0, tiled=True)  7.68 us
    pallas_call x1, Pallas kernels, unpack(): pl.pallas_call(unpack_body, grid=(channels,), in_specs=[received(spectra,...  7.36 us
    all_to_all x1, starting transfers between devices, per_device(): second = lax.all_to_all(second, AXES, 0, 0, tiled=True)  6.61 us
  transfers between devices with their start and end apart: 4, of which 3 were waited for; matrix products, arithmetic and copies ran while one was open for 0% of the time, Pallas kernels for 30%

profile of v8, /device:TPU:7, one launch (start us, length us, event | category | flops | bytes accessed | tf_op | source)
XLA Modules:
  0.0 175.2 jit_solution(4483389219963534760)
XLA Ops:
  0.0 2.7 %shard_map.39 = bf16[64,8,16,128]{3,2,1,0:T(8,128)(2,1)} custom-call(bf16[64,32,16,128]{3,2,1,0:T(8,128)(2,1)} %bitcast.6), custom_call_target="tpu_custom_call" | custom-call | tf_op jit(solution)/shard_map/pallas_call | solution.py:184
  2.7 4.5 %collective-permute-start = (bf16[64,8,16,128]{3,2,1,0:T(8,128)(2,1)}, bf16[64,8,16,128]{3,2,1,0:T(8,128)(2,1)}, u32[]{:S(2)}, u32[]{:S(2)}) collective-permute-start(bf16[64,8,16,128]{3,2,1,0:T(8,128)(2,1)} %shard_map.39), channel_id=1, source_target_pairs={{0,1},{1,2},{2,3},{3,4},{4,5},{5,6},{6,7},{7,8},{8,9},{9,10},{10,1... | collective-permute-start | bytes 6291464 | tf_op jit(solution)/shard_map/ppermute | solution.py:290
  7.2 2.5 %shard_map.40 = bf16[64,7,16,128]{3,2,1,0:T(8,128)(2,1)} custom-call(bf16[64,32,16,128]{3,2,1,0:T(8,128)(2,1)} %bitcast.7), custom_call_target="tpu_custom_call" | custom-call | tf_op jit(solution)/shard_map/pallas_call | solution.py:184
  9.7 3.0 %collective-permute-start.1 = (bf16[64,7,16,128]{3,2,1,0:T(8,128)(2,1)}, bf16[64,7,16,128]{3,2,1,0:T(8,128)(2,1)}, u32[]{:S(2)}, u32[]{:S(2)}) collective-permute-start(bf16[64,7,16,128]{3,2,1,0:T(8,128)(2,1)} %shard_map.40), channel_id=1, source_target_pairs={{0,15},{1,0},{2,1},{3,2},{4,3},{5,4},{6,5},{7,6},{8,7},{9,8},{10,9... | collective-permute-start | bytes 5505032 | tf_op jit(solution)/shard_map/ppermute | solution.py:292
  12.7 28.7 %shard_map.37 = (bf16[128,8,16,128]{3,2,1,0:T(8,128)(2,1)}, f32[64,16,16,128]{3,2,1,0:T(8,128)}) custom-call(f32[1]{0:T(128)} %bitcast.refs_0_, f32[16,1024]{1,0:T(8,128)} %refs_0_.1, bf16[4,256,512]{2,1,0:T(8,128)(2,1)} %constant.8.clone.refs_2_.refs_1_, bf16[64,32,16,128]{3,2,1,0:T(8,128)(2,1)} %bitcast.8), custom_call_target="tpu_custom_call" | custom-call | flops 274877906944 | bytes 17825792 | tf_op jit(solution)/shard_map/pallas_call | solution.py:158
  41.4 7.7 %all-to-all-start = ((bf16[128,8,16,128]{3,2,1,0:T(8,128)(2,1)}), bf16[128,8,16,128]{3,2,1,0:T(8,128)(2,1)}, u32[]{:S(2)}, u32[]{:S(2)}) async-start(bf16[128,8,16,128]{3,2,1,0:T(8,128)(2,1)} %get-tuple-element.8), calls=%async_computation | async-start | bytes 8388608 | tf_op jit(solution)/shard_map/all_to_all | solution.py:299
  49.1 9.8 %collective-permute-done.1.refs_4_ = bf16[64,7,16,128]{3,2,1,0:T(8,128)(2,1)} collective-permute-done((bf16[64,7,16,128]{3,2,1,0:T(8,128)(2,1)}, bf16[64,7,16,128]{3,2,1,0:T(8,128)(2,1)}, u32[]{:S(2)}, u32[]{:S(2)}) %collective-permute-start.1) | collective-permute-done | bytes 1835040 | tf_op jit(solution)/shard_map/ppermute | solution.py:292
  58.9 0.0 collective-permute-done.refs_3_
  58.9 14.2 %shard_map.41 = bf16[128,8,16,128]{3,2,1,0:T(8,128)(2,1)} custom-call(f32[16,1024]{1,0:T(8,128)} %refs_0_.1, bf16[4,256,512]{2,1,0:T(8,128)(2,1)} %constant.8.clone.refs_2_.refs_1_, f32[64,16,16,128]{3,2,1,0:T(8,128)} %get-tuple-element.9.refs_2_, bf16[64,8,16,128]{3,2,1,0:T(8,128)(2,1)} %collective-permute-done.refs_3_, ...), custom_call_target="tpu_custom_call" | custom-call | flops 274877906944 | bytes 17825792 | tf_op jit(solution)/shard_map/pallas_call | solution.py:158
  73.2 31.2 %all-to-all-done.ref = bf16[128,8,16,128]{3,2,1,0:T(8,128)(2,1)} async-done(((bf16[128,8,16,128]{3,2,1,0:T(8,128)(2,1)}), bf16[128,8,16,128]{3,2,1,0:T(8,128)(2,1)}, u32[]{:S(2)}, u32[]{:S(2)}) %all-to-all-start) | async-done | bytes 4194336 | tf_op jit(solution)/shard_map/all_to_all | solution.py:299
  104.4 6.6 %all-to-all-start.1 = ((bf16[128,8,16,128]{3,2,1,0:T(8,128)(2,1)}), bf16[128,8,16,128]{3,2,1,0:T(8,128)(2,1)}, u32[]{:S(2)}, u32[]{:S(2)}) async-start(bf16[128,8,16,128]{3,2,1,0:T(8,128)(2,1)} %shard_map.41), calls=%async_computation.1 | async-start | bytes 8388608 | tf_op jit(solution)/shard_map/all_to_all | solution.py:300
  111.0 7.4 %shard_map.38.refs_0_ = bf16[8,2,256,512]{3,2,1,0:T(8,128)(2,1)} custom-call(bf16[128,8,16,128]{3,2,1,0:T(8,128)(2,1)} %all-to-all-done.ref), custom_call_target="tpu_custom_call" | custom-call | flops 274877906944 | bytes 9437184 | tf_op jit(solution)/shard_map/pallas_call | solution.py:218
  118.3 44.6 %all-to-all-done.1.refs_1_ = bf16[128,8,16,128]{3,2,1,0:T(8,128)(2,1)} async-done(((bf16[128,8,16,128]{3,2,1,0:T(8,128)(2,1)}), bf16[128,8,16,128]{3,2,1,0:T(8,128)(2,1)}, u32[]{:S(2)}, u32[]{:S(2)}) %all-to-all-start.1) | async-done | bytes 4194336 | tf_op jit(solution)/shard_map/all_to_all | solution.py:300
  162.9 12.3 %shard_map.42 = f32[8,2,512,512]{3,2,1,0:T(8,128)} custom-call(bf16[8,2,256,512]{3,2,1,0:T(8,128)(2,1)} %shard_map.38.refs_0_, bf16[128,8,16,128]{3,2,1,0:T(8,128)(2,1)} %all-to-all-done.1.refs_1_), custom_call_target="tpu_custom_call" | custom-call | flops 4294967296 | bytes 26214400 | tf_op jit(solution)/shard_map/pallas_call | solution.py:263
Async XLA Ops:
  2.7 56.3 %collective-permute-start = (bf16[64,8,16,128]{3,2,1,0:T(8,128)(2,1)}, bf16[64,8,16,128]{3,2,1,0:T(8,128)(2,1)}, u32[]{:S(2)}, u32[]{:S(2)}) collective-permute-start(bf16[64,8,16,128]{3,2,1,0:T(8,128)(2,1)} %shard_map.39), channel_id=1, source_target_pairs={{0,1},{1,2},{2,3},{3,4},{4,5},{5,6},{6,7},{7,8},{8,9},{9,10},{10,1... | collective-permute-start | bytes 6291464 | tf_op jit(solution)/shard_map/ppermute | solution.py:290
  9.7 49.2 %collective-permute-start.1 = (bf16[64,7,16,128]{3,2,1,0:T(8,128)(2,1)}, bf16[64,7,16,128]{3,2,1,0:T(8,128)(2,1)}, u32[]{:S(2)}, u32[]{:S(2)}) collective-permute-start(bf16[64,7,16,128]{3,2,1,0:T(8,128)(2,1)} %shard_map.40), channel_id=1, source_target_pairs={{0,15},{1,0},{2,1},{3,2},{4,3},{5,4},{6,5},{7,6},{8,7},{9,8},{10,9... | collective-permute-start | bytes 5505032 | tf_op jit(solution)/shard_map/ppermute | solution.py:292
  41.4 63.0 %all-to-all-start = ((bf16[128,8,16,128]{3,2,1,0:T(8,128)(2,1)}), bf16[128,8,16,128]{3,2,1,0:T(8,128)(2,1)}, u32[]{:S(2)}, u32[]{:S(2)}) async-start(bf16[128,8,16,128]{3,2,1,0:T(8,128)(2,1)} %get-tuple-element.8), calls=%async_computation | async-start | bytes 8388608 | tf_op jit(solution)/shard_map/all_to_all | solution.py:299
  104.4 58.5 %all-to-all-start.1 = ((bf16[128,8,16,128]{3,2,1,0:T(8,128)(2,1)}), bf16[128,8,16,128]{3,2,1,0:T(8,128)(2,1)}, u32[]{:S(2)}, u32[]{:S(2)}) async-start(bf16[128,8,16,128]{3,2,1,0:T(8,128)(2,1)} %shard_map.41), calls=%async_computation.1 | async-start | bytes 8388608 | tf_op jit(solution)/shard_map/all_to_all | solution.py:300
